TPU v7x, 128 devices: a whole 4x4x4 slice. The times are simulated.
128 devices in a mesh: dp: 16 (over x, y), graph: 8 (over z, core).
Axes of the slice: x: 4, y: 4, z: 4, core: 2. Of those that a mesh axis runs over, the one named last changes fastest.
Arguments:
- atom_embed: bfloat16 [16, 1024, 1024], P('dp', 'graph'), may hold values from -6 to 6
- edge_embed: bfloat16 [16, 8192, 1024], P('dp', 'graph'), may hold values from -6 to 6
- source: int32 [16, 8192], P('dp', 'graph'), may hold values from 0 to 1023
- target: int32 [16, 8192], P('dp', 'graph'), may hold values from 0 to 1023
- trip_source: int32 [16, 16384], P('dp', 'graph'), may hold values from 0 to 1023
- trip_target: int32 [16, 16384], P('dp', 'graph'), may hold values from 0 to 1023
- trip_count: int32 [16, 8], P('dp', 'graph'), may hold values from 1024 to 2048, as said below
- basis_values: bfloat16 [16, 16384, 128], P('dp', 'graph'), may hold values from -6 to 6
- w_pair: bfloat16 [2048, 1024], replicated, may hold values from -0.125 to 0.125
- w_basis: bfloat16 [128, 1024], replicated, may hold values from -0.5 to 0.5
- w_out: bfloat16 [1024, 1024], replicated, may hold values from -0.1875 to 0.1875
- w_atom: bfloat16 [1024, 1024], replicated, may hold values from -0.1875 to 0.1875
- atom_cotan: bfloat16 [16, 1024, 1024], P('dp', 'graph'), may hold values from -6 to 6
- edge_cotan: bfloat16 [16, 8192, 1024], P('dp', 'graph'), may hold values from -6 to 6
Outputs:
- new_atoms: bfloat16 [16, 1024, 1024], P('dp', 'graph')
- new_edges: bfloat16 [16, 8192, 1024], P('dp', 'graph')
- grad_atoms: bfloat16 [16, 1024, 1024], P('dp', 'graph')
- grad_edges: bfloat16 [16, 8192, 1024], P('dp', 'graph')
- grad_pair: float32 [2048, 1024], P(('dp', 'graph'))
- grad_basis: float32 [128, 1024], P(('dp', 'graph'))
- grad_out: float32 [1024, 1024], P(('dp', 'graph'))
- grad_atom: float32 [1024, 1024], P(('dp', 'graph'))
Inputs may be any that keep to these rules, and one draw needn't show every extreme that they name: `trip_count`: block 0 of batch 0 is full; live slots come first in each block.
All inputs are finite; a program needn't handle non-finite values.
Results may differ from a plain program's by a relative error of at most 0.025.
Values may be sent and summed in bfloat16 or wider, within the bound.
No kernel may reach another device: no remote copies, remote signals or barrier semaphores. Data moves between devices by JAX's collectives and lax.ppermute only.
A program may use at most 128 MiB of HBM per device.

v0:
```python
import jax
import jax.numpy as jnp
from jax import lax
from jax.experimental import pallas as pl
from jax.experimental.pallas import tpu as pltpu
from jax.sharding import PartitionSpec as P

SCALE = 8.0 ** (-0.5)
BF = jnp.bfloat16
F32 = jnp.float32
COL = 512


def dot_nn(a, b):
    return lax.dot_general(a, b, (((1,), (0,)), ((), ())), preferred_element_type=F32)


def dot_nt(a, b):
    return lax.dot_general(a, b, (((1,), (1,)), ((), ())), preferred_element_type=F32)


def dot_tn(a, b):
    return lax.dot_general(a, b, (((0,), (0,)), ((), ())), preferred_element_type=F32)


def silu_slope(value):
    sigma = jax.nn.sigmoid(value)
    return sigma * (1.0 + value * (1.0 - sigma))


def fill_gather(ref, index, at=0):
    length, width = index.shape[1], 1024
    column = jnp.broadcast_to(index, (128, length)).T
    lane = lax.broadcasted_iota(jnp.int32, (length, 128), 1)
    for b in range(width // 128):
        hit = jnp.where(column == lane + b * 128, 1.0, 0.0).astype(BF)
        ref[:, at + b * 128 : at + (b + 1) * 128] = hit


def fill_scatter(ref, index):
    length, width = index.shape[1], 1024
    sub = lax.broadcasted_iota(jnp.int32, (128, length), 0)
    for b in range(width // 128):
        hit = jnp.where(sub + b * 128 == index, 1.0, 0.0).astype(BF)
        ref[b * 128 : (b + 1) * 128, :] = hit


def full(shape):
    return pl.BlockSpec(shape, lambda j: (0,) * len(shape))


def cols(rows, width=COL):
    return pl.BlockSpec((rows, width), lambda j: (0, j))


def call(body, grid, in_specs, out_specs, out_shape, scratch, flops, moved, mib, name):
    return pl.pallas_call(
        body,
        grid=grid,
        in_specs=in_specs,
        out_specs=out_specs,
        out_shape=out_shape,
        scratch_shapes=scratch,
        compiler_params=pltpu.CompilerParams(vmem_limit_bytes=mib << 20),
        cost_estimate=pl.CostEstimate(flops=flops, bytes_accessed=moved, transcendentals=0),
        name=name,
    )


STEPS = 1024 // COL


def early(rows, width=COL):
    return pl.BlockSpec((rows, width), lambda j: (0, jnp.minimum(j, STEPS - 1)))


def late(rows, width=COL):
    return pl.BlockSpec((rows, width), lambda j: (0, jnp.maximum(j - STEPS, 0)))


def prepare_body(basis, w_basis, filters, turned):
    filters[...] = dot_nn(basis[...], w_basis[...]).astype(BF)

    @pl.when(pl.program_id(0) == 0)
    def _():
        turned[...] = basis[...].T


def prepare(basis, w_basis):
    return call(
        prepare_body,
        (STEPS,),
        [full((2048, 128)), cols(128)],
        [cols(2048), full((128, 2048))],
        [jax.ShapeDtypeStruct((2048, 1024), BF), jax.ShapeDtypeStruct((128, 2048), BF)],
        [],
        int(2.15e9 * 0.6),
        6 << 20,
        60,
        "prepare",
    )(basis, w_basis)


def forward_body(*refs):
    blocks = refs[:8]
    src, dst, tin, ttg, w_pair, filters, edge, w_out = refs[8:16]
    rows_out, in_rows, slope, summed_out, new_edges, keep, give = refs[16:23]
    atoms, one_hot, gather_in, scatter_tgt, msg, rows, summed, sems = refs[23:]
    rows_copy = pltpu.make_async_copy(rows, rows_out, sems.at[0])
    summed_copy = pltpu.make_async_copy(summed, summed_out, sems.at[1])
    step = pl.program_id(0)

    @pl.when(step == 0)
    def _():
        for b in range(8):
            atoms[b * 128 : (b + 1) * 128, :] = blocks[b][...]
        for part, index in enumerate((src, dst)):
            fill_gather(one_hot, index[...])
            rows[:, part * 1024 : (part + 1) * 1024] = dot_nn(one_hot[...], atoms[...]).astype(BF)
        rows_copy.start()
        fill_gather(gather_in, tin[...])
        fill_scatter(scatter_tgt, ttg[...])

    @pl.when(step < STEPS)
    def _():
        preact = dot_nn(rows[...], w_pair[...])
        sigma = jax.nn.sigmoid(preact)
        slope[...] = (sigma * (1.0 + preact * (1.0 - sigma))).astype(BF)
        activated = (preact * sigma).astype(BF)
        for t in range(2):
            part = slice(t * 1024, (t + 1) * 1024)
            found = dot_nn(gather_in[part, :], activated).astype(BF)
            in_rows[part, :] = found
            msg[part, :] = found * filters[part, :]
        at = pl.ds(pl.multiple_of(step * COL, COL), COL)
        summed[:, at] = dot_nn(scatter_tgt[...], msg[...]).astype(BF)

    @pl.when(step == STEPS)
    def _():
        summed_copy.start()
        fill_scatter(one_hot, dst[...])

    @pl.when(step >= STEPS)
    def _():
        new = (edge[...].astype(F32) + dot_nn(summed[...], w_out[...])).astype(BF)
        new_edges[...] = new
        total = dot_nn(one_hot[...], new).astype(BF)
        keep[...] = total[:512]
        give[...] = total[512:]

    @pl.when(step == 2 * STEPS - 1)
    def _():
        rows_copy.wait()
        summed_copy.wait()


def forward(blocks, src, dst, tin, ttg, w_pair, filters, edge, w_out):
    return call(
        forward_body,
        (2 * STEPS,),
        [full((128, 1024))] * 8
        + [full((1, 1024))] * 2
        + [full((1, 2048))] * 2
        + [early(2048), early(2048), late(1024), late(1024)],
        [pl.BlockSpec(memory_space=pl.ANY), early(2048), early(1024), pl.BlockSpec(memory_space=pl.ANY)]
        + [late(1024), late(512), late(512)],
        [
            jax.ShapeDtypeStruct((1024, 2048), BF),
            jax.ShapeDtypeStruct((2048, 1024), BF),
            jax.ShapeDtypeStruct((1024, 1024), BF),
            jax.ShapeDtypeStruct((1024, 1024), BF),
            jax.ShapeDtypeStruct((1024, 1024), BF),
            jax.ShapeDtypeStruct((512, 1024), BF),
            jax.ShapeDtypeStruct((512, 1024), BF),
        ],
        [
            pltpu.VMEM((1024, 1024), BF),
            pltpu.VMEM((1024, 1024), BF),
            pltpu.VMEM((2048, 1024), BF),
            pltpu.VMEM((1024, 2048), BF),
            pltpu.VMEM((2048, COL), BF),
            pltpu.VMEM((1024, 2048), BF),
            pltpu.VMEM((1024, 1024), BF),
            pltpu.SemaphoreType.DMA((2,)),
        ],
        int(2.15e9 * 10.3),
        28 << 20,
        60,
        "forward",
    )(*blocks, src, dst, tin, ttg, w_pair, filters, edge, w_out)


def atom_body(y0, y1, y2, y3, atoms, cotan, w_atom, atom_sum, new_atoms, d_z, d_sum):
    total = y0[...].astype(F32) + y1[...].astype(F32) + y2[...].astype(F32) + y3[...].astype(F32)
    held = (total * SCALE).astype(BF)
    atom_sum[...] = held
    z = dot_nn(held, w_atom[...])
    sigma = jax.nn.sigmoid(z)
    new_atoms[...] = (atoms[...].astype(F32) + z * sigma).astype(BF)
    dz = (cotan[...].astype(F32) * (sigma * (1.0 + z * (1.0 - sigma)))).astype(BF)
    d_z[...] = dz
    d_sum[...] = dot_nt(dz, w_atom[...]).astype(BF)


def atom_update(ys, atoms, cotan, w_atom):
    return call(
        atom_body,
        (1,),
        [full((128, 1024))] * 6 + [full((1024, 1024))],
        [full((128, 1024))] * 4,
        [jax.ShapeDtypeStruct((128, 1024), BF)] * 4,
        [],
        int(2.15e9 / 4),
        5 << 20,
        14,
        "atom_update",
    )(*ys, atoms, cotan, w_atom)


def own_rows(core, even, odd, keep, give):
    even, odd = even.astype(BF), odd.astype(BF)
    keep[...] = jnp.where(core == 0, even, odd)
    give[...] = jnp.where(core == 0, odd, even)


SCALAR = pl.BlockSpec(memory_space=pltpu.SMEM)


def back_edge_body(*refs):
    blocks = refs[:8]
    core, dst, cotan, summed, atom_sum, d_z = refs[8:14]
    d_edge, keep, give = refs[14:17]
    found, gather_dst = refs[17:]

    @pl.when(pl.program_id(0) == 0)
    def _():
        fill_gather(gather_dst, dst[...])

    for b in range(8):
        found[b * 128 : (b + 1) * 128, :] = blocks[b][...]
    back = (cotan[...].astype(F32) + SCALE * dot_nn(gather_dst[...], found[...])).astype(BF)
    d_edge[...] = back
    out = dot_tn(summed[...], back).reshape(64, 2, 8, COL)
    atom = dot_tn(atom_sum[...], d_z[...]).reshape(64, 2, 8, COL)
    both = jnp.concatenate([out, atom], axis=2)
    own_rows(core[0], both[:, 0], both[:, 1], keep, give)


def edge_backward(blocks, core, dst, cotan, summed, atom_sum, d_z):
    chunks = pl.BlockSpec((64, 16, COL), lambda j: (0, 0, j))
    return call(
        back_edge_body,
        (STEPS,),
        [cols(128)] * 8
        + [SCALAR, full((1, 1024)), cols(1024), full((1024, 1024))]
        + [full((128, 1024)), cols(128)],
        [cols(1024), chunks, chunks],
        [
            jax.ShapeDtypeStruct((1024, 1024), BF),
            jax.ShapeDtypeStruct((64, 16, 1024), BF),
            jax.ShapeDtypeStruct((64, 16, 1024), BF),
        ],
        [pltpu.VMEM((1024, COL), BF), pltpu.VMEM((1024, 1024), BF)],
        int(2.15e9 * 2.2),
        12 << 20,
        40,
        "edge_backward",
    )(*blocks, core, dst, cotan, summed, atom_sum, d_z)


CHUNK = 1024 + 128
FOLD = 1024 // STEPS


def trip_body(*refs):
    core, d_summed, in_rows, slope, turned, filters, rows, tin, ttg = refs[:9]
    d_preact, keep, give = refs[9:12]
    gather_tgt, scatter_in, msg, d_filter, held, grad_basis, folded = refs[12:]
    step = pl.program_id(0)

    @pl.when(step == 0)
    def _():
        fill_gather(gather_tgt, ttg[...])
        fill_scatter(scatter_in, tin[...])

    @pl.when(step < STEPS)
    def _():
        for t in range(2):
            part = slice(t * 1024, (t + 1) * 1024)
            d_trip = dot_nn(gather_tgt[part, :], d_summed[...]).astype(BF)
            d_filter[part, :] = d_trip * in_rows[part, :]
            msg[part, :] = d_trip * filters[part, :]
        at = pl.ds(pl.multiple_of(step * COL, COL), COL)
        grad_basis[:, at] = dot_nn(turned[...], d_filter[...])
        d_active = dot_nn(scatter_in[...], msg[...])
        d_pre = (d_active * slope[...].astype(F32)).astype(BF)
        d_preact[...] = d_pre
        held[:, at] = d_pre

    @pl.when(step == STEPS)
    def _():
        for i in range(8):
            folded[pl.ds(i, 128, stride=8), :] = grad_basis[:, i * 128 : (i + 1) * 128]

    @pl.when(step >= STEPS)
    def _():
        both = dot_tn(rows[...], held[...]).reshape(64 // STEPS, 2, 16, 1024)
        at = pl.ds(pl.multiple_of((step - STEPS) * FOLD, FOLD), FOLD)
        fold = folded[at, :].reshape(64 // STEPS, 2, 8, 128)
        fold = jnp.concatenate([fold, jnp.zeros_like(fold)], axis=2)
        both = jnp.concatenate([both, fold], axis=3)
        own_rows(core[0], both[:, 0], both[:, 1], keep, give)


def own_rows(core, even, odd, keep, give):
    even, odd = even.astype(BF), odd.astype(BF)
    keep[...] = jnp.where(core == 0, even, odd)
    give[...] = jnp.where(core == 0, odd, even)


def trip_backward(core, d_summed, in_rows, slope, turned, filters, rows, tin, ttg):
    chunks = pl.BlockSpec((64 // STEPS, 16, CHUNK), lambda j: (jnp.maximum(j - STEPS, 0), 0, 0))
    return call(
        trip_body,
        (2 * STEPS,),
        [
            SCALAR,
            early(1024),
            early(2048),
            early(1024),
            full((128, 2048)),
            early(2048),
            late(1024, 2048 // STEPS),
            full((1, 2048)),
            full((1, 2048)),
        ],
        [early(1024), chunks, chunks],
        [
            jax.ShapeDtypeStruct((1024, 1024), BF),
            jax.ShapeDtypeStruct((64, 16, CHUNK), BF),
            jax.ShapeDtypeStruct((64, 16, CHUNK), BF),
        ],
        [
            pltpu.VMEM((2048, 1024), BF),
            pltpu.VMEM((1024, 2048), BF),
            pltpu.VMEM((2048, COL), BF),
            pltpu.VMEM((2048, COL), BF),
            pltpu.VMEM((1024, 1024), BF),
            pltpu.VMEM((128, 1024), F32),
            pltpu.VMEM((1024, 128), F32),
        ],
        int(2.15e9 * 6.6),
        24 << 20,
        60,
        "trip_backward",
    )(core, d_summed, in_rows, slope, turned, filters, rows, tin, ttg)


def project_body(d_edge, w_out, d_summed):
    d_summed[...] = dot_nt(d_edge[...], w_out[...]).astype(BF)


def project_back(d_edge, w_out):
    return call(
        project_body,
        (STEPS,),
        [full((1024, 1024)), pl.BlockSpec((COL, 1024), lambda j: (j, 0))],
        cols(1024),
        jax.ShapeDtypeStruct((1024, 1024), BF),
        [],
        int(2.15e9),
        6 << 20,
        24,
        "project_back",
    )(d_edge, w_out)


def atom_sums_body(d_preact, src, dst, sums, scatter):
    @pl.when(pl.program_id(0) == 0)
    def _():
        fill_scatter(scatter.at[pl.ds(0, 1024)], src[...])
        fill_scatter(scatter.at[pl.ds(1024, 1024)], dst[...])

    sums[...] = dot_nn(scatter[...], d_preact[...]).astype(BF)


def atom_sums(d_preact, src, dst):
    return call(
        atom_sums_body,
        (STEPS,),
        [cols(1024), full((1, 1024)), full((1, 1024))],
        cols(2048),
        jax.ShapeDtypeStruct((2048, 1024), BF),
        [pltpu.VMEM((2048, 1024), BF)],
        int(2.15e9 * 2),
        6 << 20,
        28,
        "atom_sums",
    )(d_preact, src, dst)


def atom_backward_body(sums, w_src, w_dst, keep, give):
    back = dot_nt(sums[:1024], w_src[...]) + dot_nt(sums[1024:], w_dst[...])
    keep[...] = back[:512].astype(BF)
    give[...] = back[512:].astype(BF)


def atom_backward(sums, w_pair):
    return call(
        atom_backward_body,
        (STEPS,),
        [
            full((2048, 1024)),
            pl.BlockSpec((COL, 1024), lambda j: (j, 0)),
            pl.BlockSpec((COL, 1024), lambda j: (STEPS + j, 0)),
        ],
        [cols(512)] * 2,
        [jax.ShapeDtypeStruct((512, 1024), BF)] * 2,
        [],
        int(2.15e9 * 2),
        10 << 20,
        26,
        "atom_backward",
    )(sums, w_pair, w_pair)


def swap_core(x):
    return lax.ppermute(x, "graph", [(i, i ^ 1) for i in range(8)])


def along_z(x, shift):
    return lax.ppermute(
        x, "graph", [(2 * z + c, 2 * ((z + shift) % 4) + c) for z in range(4) for c in range(2)]
    )


def gather_graph(x, beside=None):
    same = [along_z(x, -k) for k in (1, 2, 3)]
    if beside is not None:
        *same, beside = tie(*same, beside())
    same = [x] + same
    blocks = same + [swap_core(block) for block in same]
    return blocks, beside


def scatter_graph(keep, give):
    both = (keep.astype(F32) + swap_core(give).astype(F32)).astype(BF).reshape(4, 128, -1)
    return [both[0]] + [along_z(both[k], k) for k in (1, 2, 3)]


def add_core(keep, give):
    return keep + swap_core(give)


def spread_chunks(both):
    groups = [[i for i in range(128) if i % 2 == c] for c in range(2)]
    return lax.all_to_all(both, ("dp", "graph"), 0, 0, tiled=True, axis_index_groups=groups)


def add_chunks(spread):
    return jnp.sum(spread.astype(F32), axis=0)


def tie(*values):
    return lax.optimization_barrier(values)


def on_device(
    atom_embed,
    edge_embed,
    source,
    target,
    trip_source,
    trip_target,
    trip_count,
    basis_values,
    w_pair,
    w_basis,
    w_out,
    w_atom,
    atom_cotan,
    edge_cotan,
):
    place = lax.axis_index("graph")
    chip, core = place // 2, place % 2

    def local(index):
        owner = index // 128
        step = (owner // 2 - chip) & 3
        return (((owner & 1) ^ core) * 4 + step) * 128 + (index & 127)

    own_atoms, cotan = atom_embed[0], atom_cotan[0]
    src, dst = local(source), local(target)
    slot = lax.broadcasted_iota(jnp.int32, trip_target.shape, 1)
    tin, ttg = trip_source, jnp.where(slot < trip_count, trip_target, -1)
    basis = basis_values[0]

    blocks, (filters, turned) = gather_graph(own_atoms, lambda: prepare(basis, w_basis))
    rows, in_rows, slope, summed, new_edges, keep, give = forward(
        blocks, src, dst, tin, ttg, w_pair, filters, edge_embed[0], w_out
    )
    atom_sum, new_atoms, d_z, d_sum = atom_update(
        scatter_graph(keep, give), own_atoms, cotan, w_atom
    )
    d_edge, keep, give = edge_backward(
        gather_graph(d_sum)[0], core[None], dst, edge_cotan[0], summed, atom_sum, d_z
    )
    both = add_core(keep, give)
    d_summed, both = tie(project_back(d_edge, w_out), both)
    spread = spread_chunks(both)
    d_preact, keep, give = trip_backward(
        core[None], d_summed, in_rows, slope, turned, filters, rows, tin, ttg
    )
    d_preact, spread, keep, give = tie(d_preact, spread, keep, give)
    out_atom = add_chunks(spread)
    both = add_core(keep, give)
    sums, both, out_atom = tie(atom_sums(d_preact, src, dst), both, out_atom)
    spread = spread_chunks(both)
    back = scatter_graph(*atom_backward(sums, w_pair))
    grads_new = (cotan.astype(F32) + sum(b.astype(F32) for b in back)).astype(BF)
    pair = add_chunks(spread)
    pair_total, basis_total = pair[:, :1024], pair[:8, 1024:].reshape(1, 1024)
    out_total, atom_w_total = out_atom[:8], out_atom[8:]
    return (
        new_atoms[None],
        new_edges[None],
        grads_new[None],
        d_edge[None],
        pair_total,
        basis_total,
        out_total,
        atom_w_total,
    )


def solution(mesh):
    rows, flat = P("dp", "graph", None), P("dp", "graph")
    placed = (rows, rows, flat, flat, flat, flat, flat, rows, P(), P(), P(), P(), rows, rows)
    spread = P(("dp", "graph"), None)
    return jax.shard_map(
        on_device,
        mesh=mesh,
        in_specs=placed,
        out_specs=(rows,) * 4 + (spread,) * 4,
        check_vma=False,
    )
```

profile of v0, /device:TPU:1, one launch (start us, length us, event | category | flops | bytes accessed | tf_op | source)
XLA Modules:
  0.0 213.9 jit_solution(13825443084824281008)
XLA Ops:
  0.6 2.5 %collective-permute-start.2 = (bf16[128,1024]{1,0:T(8,128)(2,1)}, bf16[128,1024]{1,0:T(8,128)(2,1)S(1)}, u32[]{:S(2)}, u32[]{:S(2)}) collective-permute-start(bf16[128,1024]{1,0:T(8,128)(2,1)} %bitcast.16), channel_id=1, source_target_pairs={{0,2},{1,3},{2,4},{3,5},{4,6},{5,7},{6,0},{7,1},{8,10},{9,11},{10,... | collective-permute-start | bytes 786440 | tf_op jit(solution)/shard_map/ppermute | solution.py:432
  3.2 3.3 %collective-permute-start.1 = (bf16[128,1024]{1,0:T(8,128)(2,1)}, bf16[128,1024]{1,0:T(8,128)(2,1)S(1)}, u32[]{:S(2)}, u32[]{:S(2)}) collective-permute-start(bf16[128,1024]{1,0:T(8,128)(2,1)} %bitcast.17), channel_id=1, source_target_pairs={{0,4},{1,5},{2,6},{3,7},{4,0},{5,1},{6,2},{7,3},{8,12},{9,13},{10,... | collective-permute-start | bytes 786440 | tf_op jit(solution)/shard_map/ppermute | solution.py:432
  9.4 4.2 %prepare.1 = (bf16[2048,1024]{1,0:T(8,128)(2,1)}, bf16[128,2048]{1,0:T(8,128)(2,1)}) custom-call(bf16[2048,128]{1,0:T(8,128)(2,1)} %bitcast.26, bf16[128,1024]{1,0:T(8,128)(2,1)} %w_basis.1), custom_call_target="tpu_custom_call" | custom-call | flops 1290000000 | bytes 6291456 | tf_op jit(solution)/shard_map/prepare/pallas_call | solution.py:90
  13.6 4.4 %collective-permute-done.1.refs_2_ = bf16[128,1024]{1,0:T(8,128)(2,1)S(1)} collective-permute-done((bf16[128,1024]{1,0:T(8,128)(2,1)}, bf16[128,1024]{1,0:T(8,128)(2,1)S(1)}, u32[]{:S(2)}, u32[]{:S(2)}) %collective-permute-start.1) | collective-permute-done | bytes 262176 | tf_op jit(solution)/shard_map/ppermute | solution.py:432
  22.4 32.6 %forward.1 = (bf16[1024,2048]{1,0:T(8,128)(2,1)}, bf16[2048,1024]{1,0:T(8,128)(2,1)}, bf16[1024,1024]{1,0:T(8,128)(2,1)}, bf16[1024,1024]{1,0:T(8,128)(2,1)}, bf...) custom-call(bf16[128,1024]{1,0:T(8,128)(2,1)} %bitcast.20, ...), custom_call_target="tpu_custom_call" | custom-call | flops 22144999424 | bytes 29360128 | tf_op jit(solution)/shard_map/forward/pallas_call | solution.py:158
  55.6 2.7 %collective-permute-done.7 = bf16[512,1024]{1,0:T(8,128)(2,1)S(1)} collective-permute-done((bf16[512,1024]{1,0:T(8,128)(2,1)}, bf16[512,1024]{1,0:T(8,128)(2,1)S(1)}, u32[]{:S(2)}, u32[]{:S(2)}) %collective-permute-start.7) | collective-permute-done | bytes 1048608 | tf_op jit(solution)/shard_map/ppermute | solution.py:428
  58.3 1.8 add_convert_fusion.1
  60.2 1.9 collective-permute-start.10
  63.0 5.0 %collective-permute-done.10.y3 = bf16[128,1024]{1,0:T(8,128)(2,1)S(1)} collective-permute-done((bf16[128,1024]{1,0:T(8,128)(2,1)S(1)}, bf16[128,1024]{1,0:T(8,128)(2,1)S(1)}, u32[]{:S(2)}, u32[]{:S(2)}) %collective-permute-start.10) | collective-permute-done | bytes 262176 | tf_op jit(solution)/shard_map/ppermute | solution.py:432
  67.9 3.0 %collective-permute-done.9.y2 = bf16[128,1024]{1,0:T(8,128)(2,1)S(1)} collective-permute-done((bf16[128,1024]{1,0:T(8,128)(2,1)S(1)}, bf16[128,1024]{1,0:T(8,128)(2,1)S(1)}, u32[]{:S(2)}, u32[]{:S(2)}) %collective-permute-start.9) | collective-permute-done | bytes 262176 | tf_op jit(solution)/shard_map/ppermute | solution.py:432
  71.0 6.4 %collective-permute-done.8.y1 = bf16[128,1024]{1,0:T(8,128)(2,1)S(1)} collective-permute-done((bf16[128,1024]{1,0:T(8,128)(2,1)S(1)}, bf16[128,1024]{1,0:T(8,128)(2,1)S(1)}, u32[]{:S(2)}, u32[]{:S(2)}) %collective-permute-start.8) | collective-permute-done | bytes 262176 | tf_op jit(solution)/shard_map/ppermute | solution.py:432
  77.4 1.8 atom_update.1
  80.0 2.1 collective-permute-start.11
  83.4 9.9 %collective-permute-done.13.refs_3_ = bf16[128,1024]{1,0:T(8,128)(2,1)S(1)} collective-permute-done((bf16[128,1024]{1,0:T(8,128)(2,1)S(1)}, bf16[128,1024]{1,0:T(8,128)(2,1)S(1)}, u32[]{:S(2)}, u32[]{:S(2)}) %collective-permute-start.13) | collective-permute-done | bytes 262176 | tf_op jit(solution)/shard_map/ppermute | solution.py:432
  96.6 6.6 %edge_backward.1 = (bf16[1024,1024]{1,0:T(8,128)(2,1)}, bf16[64,16,1024]{2,1,0:T(8,128)(2,1)S(1)}, bf16[64,16,1024]{2,1,0:T(8,128)(2,1)S(1)}) custom-call(bf16[128,1024]{1,0:T(8,128)(2,1)S(1)} %get-tuple-element.53.refs_0_, bf16[128,1024]{1,0:T(8,128)(2,1)S(1)} %collective-permute-done.11.refs_1_, bf16[128,1024]{1,0:T(8,128)(2,1)S(1)} %collective-permute-done.12.refs_2_, ...), custom_call_target="tpu_custom_call" | custom-call | flops 4729999872 | bytes 12582912 | tf_op jit(solution)/shard_map/edge_backward/pallas_call | solution.py:251
  105.3 2.7 %project_back.1.refs_1_ = bf16[1024,1024]{1,0:T(8,128)(2,1)S(1)} custom-call(bf16[1024,1024]{1,0:T(8,128)(2,1)S(1)} %copy-done.8, bf16[1024,1024]{1,0:T(8,128)(2,1)S(1)} %copy-done.7), custom_call_target="tpu_custom_call" | custom-call | flops 2150000128 | bytes 6291456 | tf_op jit(solution)/shard_map/project_back/pallas_call | solution.py:364
  109.4 2.4 %add.51 = bf16[64,16,1024]{2,1,0:T(8,128)(2,1)} add(bf16[64,16,1024]{2,1,0:T(8,128)(2,1)S(1)} %get-tuple-element.58, bf16[64,16,1024]{2,1,0:T(8,128)(2,1)S(1)} %collective-permute-done.18) | non-fusion elementwise | flops 1048576 | bytes 6291456 | tf_op jit(solution)/shard_map/add | solution.py:452
  111.8 10.2 %all-to-all-start = ((bf16[64,16,1024]{2,1,0:T(8,128)(2,1)}), bf16[64,16,1024]{2,1,0:T(8,128)(2,1)}, u32[]{:S(2)}, u32[]{:S(2)}) async-start(bf16[64,16,1024]{2,1,0:T(8,128)(2,1)} %add.51), calls=%async_computation | async-start | bytes 4194304 | tf_op jit(solution)/shard_map/all_to_all | solution.py:457
  122.0 23.2 %trip_backward.1 = (bf16[1024,1024]{1,0:T(8,128)(2,1)}, bf16[64,16,1152]{2,1,0:T(8,128)(2,1)}, bf16[64,16,1152]{2,1,0:T(8,128)(2,1)}) custom-call(s32[1]{0:T(128)} %bitcast.7.refs_8_.refs_0_, bf16[1024,1024]{1,0:T(8,128)(2,1)} %copy-done.9, bf16[2048,1024]{1,0:T(8,128)(2,1)} %get-tuple-element.61.refs_2_, bf16[1024,1024]{1,0:T(8,128)(2,1)} %get-tuple-element.62.refs_3_, ...), custom_call_target="tpu_custom_call" | custom-call | flops 14190000128 | bytes 25165824 | tf_op jit(solution)/shard_map/trip_backward/pallas_call | solution.py:323
  145.2 4.5 %all-to-all-done = bf16[64,16,1024]{2,1,0:T(8,128)(2,1)} async-done(((bf16[64,16,1024]{2,1,0:T(8,128)(2,1)}), bf16[64,16,1024]{2,1,0:T(8,128)(2,1)}, u32[]{:S(2)}, u32[]{:S(2)}) %all-to-all-start) | async-done | bytes 2097184 | tf_op jit(solution)/shard_map/all_to_all | solution.py:457
  149.8 2.6 %collective-permute-start.19 = (bf16[64,16,1152]{2,1,0:T(8,128)(2,1)}, bf16[64,16,1152]{2,1,0:T(8,128)(2,1)S(1)}, u32[]{:S(2)}, u32[]{:S(2)}) collective-permute-start(bf16[64,16,1152]{2,1,0:T(8,128)(2,1)} %get-tuple-element.71), channel_id=1, source_target_pairs={{0,1},{1,0},{2,3},{3,2},{4,5},{5,4},{6,7},{7,6},{8,9},{9,8},{10,11... | collective-permute-start | bytes 7077896 | tf_op jit(solution)/shard_map/ppermute | solution.py:428
  152.4 1.9 convert_reduce_fusion.1
  154.4 5.9 %atom_sums.1.sums = bf16[2048,1024]{1,0:T(8,128)(2,1)S(1)} custom-call(bf16[1024,1024]{1,0:T(8,128)(2,1)S(1)} %copy-done.12, s32[1,1024]{1,0:T(1,128)S(1)} %copy-done.4, s32[1,1024]{1,0:T(1,128)S(1)} %copy-done.3), custom_call_target="tpu_custom_call" | custom-call | flops 4300000256 | bytes 6291456 | tf_op jit(solution)/shard_map/atom_sums/pallas_call | solution.py:388
  160.4 2.0 copy-done.10
  162.4 2.0 add.52
  164.4 5.5 %all-to-all-start.1 = ((bf16[64,16,1152]{2,1,0:T(8,128)(2,1)}), bf16[64,16,1152]{2,1,0:T(8,128)(2,1)S(1)}, u32[]{:S(2)}, u32[]{:S(2)}) async-start(bf16[64,16,1152]{2,1,0:T(8,128)(2,1)} %add.52), calls=%async_computation.1 | async-start | bytes 4718592 | tf_op jit(solution)/shard_map/all_to_all | solution.py:457
  169.8 2.2 %copy-done.5 = bf16[2048,1024]{1,0:T(8,128)(2,1)S(1)} copy-done((bf16[2048,1024]{1,0:T(8,128)(2,1)S(1)}, bf16[2048,1024]{1,0:T(8,128)(2,1)}, u32[]{:S(2)}) %copy-start.5) | copy-done | bytes 4194328
  172.0 2.2 %copy-done.11 = bf16[2048,1024]{1,0:T(8,128)(2,1)S(1)} copy-done((bf16[2048,1024]{1,0:T(8,128)(2,1)S(1)}, bf16[2048,1024]{1,0:T(8,128)(2,1)}, u32[]{:S(2)}) %copy-start.11) | copy-done | bytes 4194328
  174.2 4.9 %atom_backward.1 = (bf16[512,1024]{1,0:T(8,128)(2,1)S(1)}, bf16[512,1024]{1,0:T(8,128)(2,1)S(1)}) custom-call(bf16[2048,1024]{1,0:T(8,128)(2,1)S(1)} %copy-done.11, bf16[2048,1024]{1,0:T(8,128)(2,1)S(1)} %copy-done.5, bf16[2048,1024]{1,0:T(8,128)(2,1)S(1)} %copy-done.5), custom_call_target="tpu_custom_call" | custom-call | flops 4300000256 | bytes 10485760 | tf_op jit(solution)/shard_map/atom_backward/pallas_call | solution.py:409
  179.5 2.4 %collective-permute-done.20 = bf16[512,1024]{1,0:T(8,128)(2,1)S(1)} collective-permute-done((bf16[512,1024]{1,0:T(8,128)(2,1)S(1)}, bf16[512,1024]{1,0:T(8,128)(2,1)S(1)}, u32[]{:S(2)}, u32[]{:S(2)}) %collective-permute-start.20) | collective-permute-done | bytes 1048608 | tf_op jit(solution)/shard_map/ppermute | solution.py:428
  187.3 16.5 %collective-permute-done.21 = bf16[128,1024]{1,0:T(8,128)(2,1)S(1)} collective-permute-done((bf16[128,1024]{1,0:T(8,128)(2,1)S(1)}, bf16[128,1024]{1,0:T(8,128)(2,1)S(1)}, u32[]{:S(2)}, u32[]{:S(2)}) %collective-permute-start.21) | collective-permute-done | bytes 262176 | tf_op jit(solution)/shard_map/ppermute | solution.py:432
  203.8 6.4 %collective-permute-done.23 = bf16[128,1024]{1,0:T(8,128)(2,1)S(1)} collective-permute-done((bf16[128,1024]{1,0:T(8,128)(2,1)S(1)}, bf16[128,1024]{1,0:T(8,128)(2,1)S(1)}, u32[]{:S(2)}, u32[]{:S(2)}) %collective-permute-start.23) | collective-permute-done | bytes 262176 | tf_op jit(solution)/shard_map/ppermute | solution.py:432
  (92 shorter events, 26.3 us)
Async XLA Ops:
  0.6 13.0 %collective-permute-start.2 = (bf16[128,1024]{1,0:T(8,128)(2,1)}, bf16[128,1024]{1,0:T(8,128)(2,1)S(1)}, u32[]{:S(2)}, u32[]{:S(2)}) collective-permute-start(bf16[128,1024]{1,0:T(8,128)(2,1)} %bitcast.16), channel_id=1, source_target_pairs={{0,2},{1,3},{2,4},{3,5},{4,6},{5,7},{6,0},{7,1},{8,10},{9,11},{10,... | collective-permute-start | bytes 786440 | tf_op jit(solution)/shard_map/ppermute | solution.py:432
  3.2 14.8 %collective-permute-start.1 = (bf16[128,1024]{1,0:T(8,128)(2,1)}, bf16[128,1024]{1,0:T(8,128)(2,1)S(1)}, u32[]{:S(2)}, u32[]{:S(2)}) collective-permute-start(bf16[128,1024]{1,0:T(8,128)(2,1)} %bitcast.17), channel_id=1, source_target_pairs={{0,4},{1,5},{2,6},{3,7},{4,0},{5,1},{6,2},{7,3},{8,12},{9,13},{10,... | collective-permute-start | bytes 786440 | tf_op jit(solution)/shard_map/ppermute | solution.py:432
  6.5 11.5 %collective-permute-start = (bf16[128,1024]{1,0:T(8,128)(2,1)}, bf16[128,1024]{1,0:T(8,128)(2,1)S(1)}, u32[]{:S(2)}, u32[]{:S(2)}) collective-permute-start(bf16[128,1024]{1,0:T(8,128)(2,1)} %bitcast.18), channel_id=1, source_target_pairs={{0,6},{1,7},{2,0},{3,1},{4,2},{5,3},{6,4},{7,5},{8,14},{9,15},{10,... | collective-permute-start | bytes 786440 | tf_op jit(solution)/shard_map/ppermute | solution.py:432
  7.2 14.3 %collective-permute-start.3 = (bf16[128,1024]{1,0:T(8,128)(2,1)}, bf16[128,1024]{1,0:T(8,128)(2,1)S(1)}, u32[]{:S(2)}, u32[]{:S(2)}) collective-permute-start(bf16[128,1024]{1,0:T(8,128)(2,1)} %bitcast.19), channel_id=1, source_target_pairs={{0,1},{1,0},{2,3},{3,2},{4,5},{5,4},{6,7},{7,6},{8,9},{9,8},{10,11... | collective-permute-start | bytes 786440 | tf_op jit(solution)/shard_map/ppermute | solution.py:428
  18.0 3.5 %collective-permute-start.4 = (bf16[128,1024]{1,0:T(8,128)(2,1)S(1)}, bf16[128,1024]{1,0:T(8,128)(2,1)S(1)}, u32[]{:S(2)}, u32[]{:S(2)}) collective-permute-start(bf16[128,1024]{1,0:T(8,128)(2,1)S(1)} %collective-permute-done.refs_1_), channel_id=1, source_target_pairs={{0,1},{1,0},{2,3},{3,2},{4,5},{5,4},{6,7},{7,6},{8,9},{9,8},{10,11... | collective-permute-start | bytes 786440 | tf_op jit(solution)/shard_map/ppermute | solution.py:428
  19.6 1.8 collective-permute-start.5
  19.7 1.8 collective-permute-start.6
  55.1 3.2 %collective-permute-start.7 = (bf16[512,1024]{1,0:T(8,128)(2,1)}, bf16[512,1024]{1,0:T(8,128)(2,1)S(1)}, u32[]{:S(2)}, u32[]{:S(2)}) collective-permute-start(bf16[512,1024]{1,0:T(8,128)(2,1)} %get-tuple-element.50), channel_id=1, source_target_pairs={{0,1},{1,0},{2,3},{3,2},{4,5},{5,4},{6,7},{7,6},{8,9},{9,8},{10,11... | collective-permute-start | bytes 3145736 | tf_op jit(solution)/shard_map/ppermute | solution.py:428
  58.3 19.1 %copy-start = (bf16[1024,1024]{1,0:T(8,128)(2,1)S(1)}, bf16[1024,1024]{1,0:T(8,128)(2,1)}, u32[]{:S(2)}) copy-start(bf16[1024,1024]{1,0:T(8,128)(2,1)} %w_atom.1) | copy-start | bytes 6291460
  58.3 19.1 %copy-start.1 = (bf16[1,128,1024]{2,1,0:T(8,128)(2,1)S(1)}, bf16[1,128,1024]{2,1,0:T(8,128)(2,1)}, u32[]{:S(2)}) copy-start(bf16[1,128,1024]{2,1,0:T(8,128)(2,1)} %param.26) | copy-start | bytes 786436
  58.3 19.1 %copy-start.2 = (bf16[1,128,1024]{2,1,0:T(8,128)(2,1)S(1)}, bf16[1,128,1024]{2,1,0:T(8,128)(2,1)}, u32[]{:S(2)}) copy-start(bf16[1,128,1024]{2,1,0:T(8,128)(2,1)} %param.14) | copy-start | bytes 786436
  60.0 36.6 %copy-start.13 = (bf16[1024,1024]{1,0:T(8,128)(2,1)S(1)}, bf16[1024,1024]{1,0:T(8,128)(2,1)}, u32[]{:S(2)}) copy-start(bf16[1024,1024]{1,0:T(8,128)(2,1)} %get-tuple-element.54.refs_11_) | copy-start | bytes 6291460
  60.1 36.5 %copy-start.3 = (s32[1,1024]{1,0:T(1,128)S(1)}, s32[1,1024]{1,0:T(1,128)}, u32[]{:S(2)}) copy-start(s32[1,1024]{1,0:T(1,128)} %get-tuple-element.87.refs_9_.dst) | copy-start | bytes 12292
  60.1 36.5 %copy-start.6 = (bf16[1,1024,1024]{2,1,0:T(8,128)(2,1)S(1)}, bf16[1,1024,1024]{2,1,0:T(8,128)(2,1)}, u32[]{:S(2)}) copy-start(bf16[1,1024,1024]{2,1,0:T(8,128)(2,1)} %param.27) | copy-start | bytes 6291460
  60.2 7.8 %collective-permute-start.10 = (bf16[128,1024]{1,0:T(8,128)(2,1)S(1)}, bf16[128,1024]{1,0:T(8,128)(2,1)S(1)}, u32[]{:S(2)}, u32[]{:S(2)}) collective-permute-start(bf16[128,1024]{1,0:T(8,128)(2,1)S(1)} %get-tuple-element.81), channel_id=1, source_target_pairs={{0,6},{1,7},{2,0},{3,1},{4,2},{5,3},{6,4},{7,5},{8,14},{9,15},{10,... | collective-permute-start | bytes 786440 | tf_op jit(solution)/shard_map/ppermute | solution.py:432
  62.0 8.9 %collective-permute-start.9 = (bf16[128,1024]{1,0:T(8,128)(2,1)S(1)}, bf16[128,1024]{1,0:T(8,128)(2,1)S(1)}, u32[]{:S(2)}, u32[]{:S(2)}) collective-permute-start(bf16[128,1024]{1,0:T(8,128)(2,1)S(1)} %get-tuple-element.82), channel_id=1, source_target_pairs={{0,4},{1,5},{2,6},{3,7},{4,0},{5,1},{6,2},{7,3},{8,12},{9,13},{10,... | collective-permute-start | bytes 786440 | tf_op jit(solution)/shard_map/ppermute | solution.py:432
  62.9 14.5 %collective-permute-start.8 = (bf16[128,1024]{1,0:T(8,128)(2,1)S(1)}, bf16[128,1024]{1,0:T(8,128)(2,1)S(1)}, u32[]{:S(2)}, u32[]{:S(2)}) collective-permute-start(bf16[128,1024]{1,0:T(8,128)(2,1)S(1)} %get-tuple-element.83), channel_id=1, source_target_pairs={{0,2},{1,3},{2,4},{3,5},{4,6},{5,7},{6,0},{7,1},{8,10},{9,11},{10,... | collective-permute-start | bytes 786440 | tf_op jit(solution)/shard_map/ppermute | solution.py:432
  79.1 14.2 %collective-permute-start.13 = (bf16[128,1024]{1,0:T(8,128)(2,1)S(1)}, bf16[128,1024]{1,0:T(8,128)(2,1)S(1)}, u32[]{:S(2)}, u32[]{:S(2)}) collective-permute-start(bf16[128,1024]{1,0:T(8,128)(2,1)S(1)} %get-tuple-element.53.refs_0_), channel_id=1, source_target_pairs={{0,2},{1,3},{2,4},{3,5},{4,6},{5,7},{6,0},{7,1},{8,10},{9,11},{10,... | collective-permute-start | bytes 786440 | tf_op jit(solution)/shard_map/ppermute | solution.py:432
  79.1 15.6 %collective-permute-start.12 = (bf16[128,1024]{1,0:T(8,128)(2,1)S(1)}, bf16[128,1024]{1,0:T(8,128)(2,1)S(1)}, u32[]{:S(2)}, u32[]{:S(2)}) collective-permute-start(bf16[128,1024]{1,0:T(8,128)(2,1)S(1)} %get-tuple-element.53.refs_0_), channel_id=1, source_target_pairs={{0,4},{1,5},{2,6},{3,7},{4,0},{5,1},{6,2},{7,3},{8,12},{9,13},{10,... | collective-permute-start | bytes 786440 | tf_op jit(solution)/shard_map/ppermute | solution.py:432
  80.0 14.7 %collective-permute-start.11 = (bf16[128,1024]{1,0:T(8,128)(2,1)S(1)}, bf16[128,1024]{1,0:T(8,128)(2,1)S(1)}, u32[]{:S(2)}, u32[]{:S(2)}) collective-permute-start(bf16[128,1024]{1,0:T(8,128)(2,1)S(1)} %get-tuple-element.53.refs_0_), channel_id=1, source_target_pairs={{0,6},{1,7},{2,0},{3,1},{4,2},{5,3},{6,4},{7,5},{8,14},{9,15},{10,... | collective-permute-start | bytes 786440 | tf_op jit(solution)/shard_map/ppermute | solution.py:432
  82.1 13.2 %collective-permute-start.14 = (bf16[128,1024]{1,0:T(8,128)(2,1)S(1)}, bf16[128,1024]{1,0:T(8,128)(2,1)S(1)}, u32[]{:S(2)}, u32[]{:S(2)}) collective-permute-start(bf16[128,1024]{1,0:T(8,128)(2,1)S(1)} %get-tuple-element.53.refs_0_), channel_id=1, source_target_pairs={{0,1},{1,0},{2,3},{3,2},{4,5},{5,4},{6,7},{7,6},{8,9},{9,8},{10,11... | collective-permute-start | bytes 786440 | tf_op jit(solution)/shard_map/ppermute | solution.py:428
  93.4 2.5 %collective-permute-start.17 = (bf16[128,1024]{1,0:T(8,128)(2,1)S(1)}, bf16[128,1024]{1,0:T(8,128)(2,1)S(1)}, u32[]{:S(2)}, u32[]{:S(2)}) collective-permute-start(bf16[128,1024]{1,0:T(8,128)(2,1)S(1)} %collective-permute-done.13.refs_3_), channel_id=1, source_target_pairs={{0,1},{1,0},{2,3},{3,2},{4,5},{5,4},{6,7},{7,6},{8,9},{9,8},{10,11... | collective-permute-start | bytes 786440 | tf_op jit(solution)/shard_map/ppermute | solution.py:428
  94.7 1.5 collective-permute-start.16
  94.7 1.9 collective-permute-start.15
  103.3 6.1 %collective-permute-start.18 = (bf16[64,16,1024]{2,1,0:T(8,128)(2,1)S(1)}, bf16[64,16,1024]{2,1,0:T(8,128)(2,1)S(1)}, u32[]{:S(2)}, u32[]{:S(2)}) collective-permute-start(bf16[64,16,1024]{2,1,0:T(8,128)(2,1)S(1)} %get-tuple-element.59), channel_id=1, source_target_pairs={{0,1},{1,0},{2,3},{3,2},{4,5},{5,4},{6,7},{7,6},{8,9},{9,8},{10,11... | collective-permute-start | bytes 6291464 | tf_op jit(solution)/shard_map/ppermute | solution.py:428
  111.8 38.0 %all-to-all-start = ((bf16[64,16,1024]{2,1,0:T(8,128)(2,1)}), bf16[64,16,1024]{2,1,0:T(8,128)(2,1)}, u32[]{:S(2)}, u32[]{:S(2)}) async-start(bf16[64,16,1024]{2,1,0:T(8,128)(2,1)} %add.51), calls=%async_computation | async-start | bytes 4194304 | tf_op jit(solution)/shard_map/all_to_all | solution.py:457
  149.8 12.6 %collective-permute-start.19 = (bf16[64,16,1152]{2,1,0:T(8,128)(2,1)}, bf16[64,16,1152]{2,1,0:T(8,128)(2,1)S(1)}, u32[]{:S(2)}, u32[]{:S(2)}) collective-permute-start(bf16[64,16,1152]{2,1,0:T(8,128)(2,1)} %get-tuple-element.71), channel_id=1, source_target_pairs={{0,1},{1,0},{2,3},{3,2},{4,5},{5,4},{6,7},{7,6},{8,9},{9,8},{10,11... | collective-permute-start | bytes 7077896 | tf_op jit(solution)/shard_map/ppermute | solution.py:428
  164.4 47.8 %all-to-all-start.1 = ((bf16[64,16,1152]{2,1,0:T(8,128)(2,1)}), bf16[64,16,1152]{2,1,0:T(8,128)(2,1)S(1)}, u32[]{:S(2)}, u32[]{:S(2)}) async-start(bf16[64,16,1152]{2,1,0:T(8,128)(2,1)} %add.52), calls=%async_computation.1 | async-start | bytes 4718592 | tf_op jit(solution)/shard_map/all_to_all | solution.py:457
  179.1 2.7 %collective-permute-start.20 = (bf16[512,1024]{1,0:T(8,128)(2,1)S(1)}, bf16[512,1024]{1,0:T(8,128)(2,1)S(1)}, u32[]{:S(2)}, u32[]{:S(2)}) collective-permute-start(bf16[512,1024]{1,0:T(8,128)(2,1)S(1)} %get-tuple-element.75), channel_id=1, source_target_pairs={{0,1},{1,0},{2,3},{3,2},{4,5},{5,4},{6,7},{7,6},{8,9},{9,8},{10,11... | collective-permute-start | bytes 3145736 | tf_op jit(solution)/shard_map/ppermute | solution.py:428
  182.3 21.5 %collective-permute-start.21 = (bf16[128,1024]{1,0:T(8,128)(2,1)S(1)}, bf16[128,1024]{1,0:T(8,128)(2,1)S(1)}, u32[]{:S(2)}, u32[]{:S(2)}) collective-permute-start(bf16[128,1024]{1,0:T(8,128)(2,1)S(1)} %get-tuple-element.78), channel_id=1, source_target_pairs={{0,2},{1,3},{2,4},{3,5},{4,6},{5,7},{6,0},{7,1},{8,10},{9,11},{10,... | collective-permute-start | bytes 786440 | tf_op jit(solution)/shard_map/ppermute | solution.py:432
  183.7 26.5 %collective-permute-start.23 = (bf16[128,1024]{1,0:T(8,128)(2,1)S(1)}, bf16[128,1024]{1,0:T(8,128)(2,1)S(1)}, u32[]{:S(2)}, u32[]{:S(2)}) collective-permute-start(bf16[128,1024]{1,0:T(8,128)(2,1)S(1)} %get-tuple-element.79), channel_id=1, source_target_pairs={{0,6},{1,7},{2,0},{3,1},{4,2},{5,3},{6,4},{7,5},{8,14},{9,15},{10,... | collective-permute-start | bytes 786440 | tf_op jit(solution)/shard_map/ppermute | solution.py:432
  185.0 26.2 %collective-permute-start.22 = (bf16[128,1024]{1,0:T(8,128)(2,1)S(1)}, bf16[128,1024]{1,0:T(8,128)(2,1)S(1)}, u32[]{:S(2)}, u32[]{:S(2)}) collective-permute-start(bf16[128,1024]{1,0:T(8,128)(2,1)S(1)} %get-tuple-element.80), channel_id=1, source_target_pairs={{0,4},{1,5},{2,6},{3,7},{4,0},{5,1},{6,2},{7,3},{8,12},{9,13},{10,... | collective-permute-start | bytes 786440 | tf_op jit(solution)/shard_map/ppermute | solution.py:432
  (19 other events, 94.5 us)
where the time goes:
time: 217 us; the launch traced here: 214 us
  Pallas kernels  82 us (38%)
  waiting for transfers between devices  63.6 us (29%)
  starting transfers between devices  43.2 us (20%)
  local copies, waits for them, and re-layouts  12.2 us (6%)
  other arithmetic  11.1 us (5%)
    ppermute x12, waiting for transfers between devices, along_z(): lax.ppermute(x, 'graph', [(2 * z + c, 2 * ((z + shift) % 4) + c) for z in...  52.7 us
    pallas_call x1, Pallas kernels, forward(): call(forward_body, (2 * STEPS,), [full((128, 1024))] * 8 + [full((1, 1024...  32.6 us
    pallas_call x1, Pallas kernels, trip_backward(): call(trip_body, (2 * STEPS,), [SCALAR, early(1024), early(2048), early(10...  23.2 us
    ppermute x12, starting transfers between devices, along_z(): lax.ppermute(x, 'graph', [(2 * z + c, 2 * ((z + shift) % 4) + c) for z in...  16.7 us
    all_to_all x2, starting transfers between devices, spread_chunks(): lax.all_to_all(both, ('dp', 'graph'), 0, 0, tiled=True, axis_index_groups...  15.7 us
    ppermute x12, starting transfers between devices, swap_core(): return lax.ppermute(x, 'graph', [(i, i ^ 1) for i in range(8)])  10.9 us
    unnamed x50, local copies, waits for them, and re-layouts  10.2 us
    pallas_call x1, Pallas kernels, edge_backward(): call(back_edge_body, (STEPS,), [cols(128)] * 8 + [SCALAR, full((1, 1024))...  6.61 us
  transfers between devices with their start and end apart: 26, of which 14 were waited for; matrix products, arithmetic and copies ran while one was open for 2% of the time, Pallas kernels for 19%

commit v1 on v0

--- a/solution.py
+++ b/solution.py
@@ -270,35 +270,36 @@
 
 CHUNK = 1024 + 128
 FOLD = 1024 // STEPS
+PART = 2048 // STEPS
 
 
 def trip_body(*refs):
-    core, d_summed, in_rows, slope, turned, filters, rows, tin, ttg = refs[:9]
-    d_preact, keep, give = refs[9:12]
-    gather_tgt, scatter_in, msg, d_filter, held, grad_basis, folded = refs[12:]
+    core, d_summed, in_rows, slope, turned, filters, rows, tin, ttg, src, dst = refs[:11]
+    sums, keep, give = refs[11:14]
+    one_hot, scatter_in, msg, d_filter, held, grad_basis, folded = refs[14:]
     step = pl.program_id(0)
 
     @pl.when(step == 0)
     def _():
-        fill_gather(gather_tgt, ttg[...])
+        fill_gather(one_hot, ttg[...])
         fill_scatter(scatter_in, tin[...])
 
     @pl.when(step < STEPS)
     def _():
         for t in range(2):
             part = slice(t * 1024, (t + 1) * 1024)
-            d_trip = dot_nn(gather_tgt[part, :], d_summed[...]).astype(BF)
+            d_trip = dot_nn(one_hot[part, :], d_summed[...]).astype(BF)
             d_filter[part, :] = d_trip * in_rows[part, :]
             msg[part, :] = d_trip * filters[part, :]
         at = pl.ds(pl.multiple_of(step * COL, COL), COL)
         grad_basis[:, at] = dot_nn(turned[...], d_filter[...])
         d_active = dot_nn(scatter_in[...], msg[...])
-        d_pre = (d_active * slope[...].astype(F32)).astype(BF)
-        d_preact[...] = d_pre
-        held[:, at] = d_pre
+        held[:, at] = (d_active * slope[...].astype(F32)).astype(BF)
 
     @pl.when(step == STEPS)
     def _():
+        fill_scatter(one_hot.at[pl.ds(0, 1024)], src[...])
+        fill_scatter(one_hot.at[pl.ds(1024, 1024)], dst[...])
         for i in range(8):
             folded[pl.ds(i, 128, stride=8), :] = grad_basis[:, i * 128 : (i + 1) * 128]
 
@@ -310,6 +311,8 @@
         fold = jnp.concatenate([fold, jnp.zeros_like(fold)], axis=2)
         both = jnp.concatenate([both, fold], axis=3)
         own_rows(core[0], both[:, 0], both[:, 1], keep, give)
+        at = pl.ds(pl.multiple_of((step - STEPS) * PART, PART), PART)
+        sums[...] = dot_nn(one_hot[at, :], held[...]).astype(BF)
 
 
 def own_rows(core, even, odd, keep, give):
@@ -318,7 +321,7 @@
     give[...] = jnp.where(core == 0, odd, even)
 
 
-def trip_backward(core, d_summed, in_rows, slope, turned, filters, rows, tin, ttg):
+def trip_backward(core, d_summed, in_rows, slope, turned, filters, rows, tin, ttg, src, dst):
     chunks = pl.BlockSpec((64 // STEPS, 16, CHUNK), lambda j: (jnp.maximum(j - STEPS, 0), 0, 0))
     return call(
         trip_body,
@@ -333,10 +336,12 @@
             late(1024, 2048 // STEPS),
             full((1, 2048)),
             full((1, 2048)),
-        ],
-        [early(1024), chunks, chunks],
-        [
-            jax.ShapeDtypeStruct((1024, 1024), BF),
+            full((1, 1024)),
+            full((1, 1024)),
+        ],
+        [pl.BlockSpec((PART, 1024), lambda j: (jnp.maximum(j - STEPS, 0), 0)), chunks, chunks],
+        [
+            jax.ShapeDtypeStruct((2048, 1024), BF),
             jax.ShapeDtypeStruct((64, 16, CHUNK), BF),
             jax.ShapeDtypeStruct((64, 16, CHUNK), BF),
         ],
@@ -349,11 +354,11 @@
             pltpu.VMEM((128, 1024), F32),
             pltpu.VMEM((1024, 128), F32),
         ],
-        int(2.15e9 * 6.6),
+        int(2.15e9 * 8.6),
         24 << 20,
         60,
         "trip_backward",
-    )(core, d_summed, in_rows, slope, turned, filters, rows, tin, ttg)
+    )(core, d_summed, in_rows, slope, turned, filters, rows, tin, ttg, src, dst)
 
 
 def project_body(d_edge, w_out, d_summed):
@@ -375,30 +380,6 @@
     )(d_edge, w_out)
 
 
-def atom_sums_body(d_preact, src, dst, sums, scatter):
-    @pl.when(pl.program_id(0) == 0)
-    def _():
-        fill_scatter(scatter.at[pl.ds(0, 1024)], src[...])
-        fill_scatter(scatter.at[pl.ds(1024, 1024)], dst[...])
-
-    sums[...] = dot_nn(scatter[...], d_preact[...]).astype(BF)
-
-
-def atom_sums(d_preact, src, dst):
-    return call(
-        atom_sums_body,
-        (STEPS,),
-        [cols(1024), full((1, 1024)), full((1, 1024))],
-        cols(2048),
-        jax.ShapeDtypeStruct((2048, 1024), BF),
-        [pltpu.VMEM((2048, 1024), BF)],
-        int(2.15e9 * 2),
-        6 << 20,
-        28,
-        "atom_sums",
-    )(d_preact, src, dst)
-
-
 def atom_backward_body(sums, w_src, w_dst, keep, give):
     back = dot_nt(sums[:1024], w_src[...]) + dot_nt(sums[1024:], w_dst[...])
     keep[...] = back[:512].astype(BF)
@@ -419,7 +400,7 @@
         [],
         int(2.15e9 * 2),
         10 << 20,
-        26,
+        60,
         "atom_backward",
     )(sums, w_pair, w_pair)
 
@@ -459,6 +440,20 @@
 
 def add_chunks(spread):
     return jnp.sum(spread.astype(F32), axis=0)
+
+
+def spread_plane(both):
+    return lax.all_to_all(both, "dp", 0, 0, tiled=True)
+
+
+def add_plane(spread):
+    return jnp.sum(spread.reshape(16, 4, 16, -1).astype(F32), axis=0).astype(BF)
+
+
+def add_line(plane):
+    groups = [[2 * z + c for z in range(4)] for c in range(2)]
+    last = lax.all_to_all(plane, "graph", 0, 0, tiled=True, axis_index_groups=groups)
+    return jnp.sum(last.astype(F32), axis=0)
 
 
 def tie(*values):
@@ -508,17 +503,17 @@
     both = add_core(keep, give)
     d_summed, both = tie(project_back(d_edge, w_out), both)
     spread = spread_chunks(both)
-    d_preact, keep, give = trip_backward(
-        core[None], d_summed, in_rows, slope, turned, filters, rows, tin, ttg
-    )
-    d_preact, spread, keep, give = tie(d_preact, spread, keep, give)
+    sums, keep, give = trip_backward(
+        core[None], d_summed, in_rows, slope, turned, filters, rows, tin, ttg, src, dst
+    )
+    sums, spread, keep, give = tie(sums, spread, keep, give)
     out_atom = add_chunks(spread)
     both = add_core(keep, give)
-    sums, both, out_atom = tie(atom_sums(d_preact, src, dst), both, out_atom)
-    spread = spread_chunks(both)
+    sums, both, out_atom = tie(sums, both, out_atom)
+    spread = spread_plane(both)
     back = scatter_graph(*atom_backward(sums, w_pair))
     grads_new = (cotan.astype(F32) + sum(b.astype(F32) for b in back)).astype(BF)
-    pair = add_chunks(spread)
+    pair = add_line(add_plane(spread))
     pair_total, basis_total = pair[:, :1024], pair[:8, 1024:].reshape(1, 1024)
     out_total, atom_w_total = out_atom[:8], out_atom[8:]
     return (

time: 217 us -> 215 us (level)
  the two profiles are of different devices: /device:TPU:1 before, /device:TPU:0 now
where the time goes in v1:
time: 215 us; the launch traced here: 212 us
  Pallas kernels  85 us (40%)
  waiting for transfers between devices  62.8 us (29%)
  starting transfers between devices  41.5 us (19%)
  other arithmetic  14 us (7%)
  local copies, waits for them, and re-layouts  6.66 us (3%)
    pallas_call x1, Pallas kernels, forward(): call(forward_body, (2 * STEPS,), [full((128, 1024))] * 8 + [full((1, 1024...  32.6 us
    ppermute x12, waiting for transfers between devices, along_z(): lax.ppermute(x, 'graph', [(2 * z + c, 2 * ((z + shift) % 4) + c) for z in...  31.2 us
    pallas_call x1, Pallas kernels, trip_backward(): call(trip_body, (2 * STEPS,), [SCALAR, early(1024), early(2048), early(10...  28.5 us
    ppermute x12, starting transfers between devices, along_z(): lax.ppermute(x, 'graph', [(2 * z + c, 2 * ((z + shift) % 4) + c) for z in...  19.1 us
    all_to_all x1, waiting for transfers between devices, spread_plane(): return lax.all_to_all(both, 'dp', 0, 0, tiled=True)  14.1 us
    ppermute x12, waiting for transfers between devices, swap_core(): return lax.ppermute(x, 'graph', [(i, i ^ 1) for i in range(8)])  11.8 us
    all_to_all x1, starting transfers between devices, spread_chunks(): lax.all_to_all(both, ('dp', 'graph'), 0, 0, tiled=True, axis_index_groups...  10.2 us
    pallas_call x1, Pallas kernels, atom_backward(): call(atom_backward_body, (STEPS,), [full((2048, 1024)), pl.BlockSpec((COL...  8.49 us
  transfers between devices with their start and end apart: 27, of which 15 were waited for; matrix products, arithmetic and copies ran while one was open for 4% of the time, Pallas kernels for 21%

profile of v1, /device:TPU:0, one launch (start us, length us, event | category | flops | bytes accessed | tf_op | source)
XLA Modules:
  0.0 211.6 jit_solution(6286265506869912129)
XLA Ops:
  0.6 2.1 collective-permute-start.2
  2.7 3.6 %collective-permute-start.1 = (bf16[128,1024]{1,0:T(8,128)(2,1)}, bf16[128,1024]{1,0:T(8,128)(2,1)S(1)}, u32[]{:S(2)}, u32[]{:S(2)}) collective-permute-start(bf16[128,1024]{1,0:T(8,128)(2,1)} %bitcast.18), channel_id=1, source_target_pairs={{0,4},{1,5},{2,6},{3,7},{4,0},{5,1},{6,2},{7,3},{8,12},{9,13},{10,... | collective-permute-start | bytes 786440 | tf_op jit(solution)/shard_map/ppermute | solution.py:413
  8.0 4.3 %prepare.1 = (bf16[2048,1024]{1,0:T(8,128)(2,1)}, bf16[128,2048]{1,0:T(8,128)(2,1)}) custom-call(bf16[2048,128]{1,0:T(8,128)(2,1)} %bitcast.28, bf16[128,1024]{1,0:T(8,128)(2,1)} %w_basis.1), custom_call_target="tpu_custom_call" | custom-call | flops 1290000000 | bytes 6291456 | tf_op jit(solution)/shard_map/prepare/pallas_call | solution.py:90
  12.3 5.9 %collective-permute-done.1.refs_2_ = bf16[128,1024]{1,0:T(8,128)(2,1)S(1)} collective-permute-done((bf16[128,1024]{1,0:T(8,128)(2,1)}, bf16[128,1024]{1,0:T(8,128)(2,1)S(1)}, u32[]{:S(2)}, u32[]{:S(2)}) %collective-permute-start.1) | collective-permute-done | bytes 262176 | tf_op jit(solution)/shard_map/ppermute | solution.py:413
  21.2 32.6 %forward.1 = (bf16[1024,2048]{1,0:T(8,128)(2,1)}, bf16[2048,1024]{1,0:T(8,128)(2,1)}, bf16[1024,1024]{1,0:T(8,128)(2,1)}, bf16[1024,1024]{1,0:T(8,128)(2,1)}, bf...) custom-call(bf16[128,1024]{1,0:T(8,128)(2,1)} %bitcast.21, ...), custom_call_target="tpu_custom_call" | custom-call | flops 22144999424 | bytes 29360128 | tf_op jit(solution)/shard_map/forward/pallas_call | solution.py:158
  54.5 2.5 %collective-permute-done.7 = bf16[512,1024]{1,0:T(8,128)(2,1)S(1)} collective-permute-done((bf16[512,1024]{1,0:T(8,128)(2,1)}, bf16[512,1024]{1,0:T(8,128)(2,1)S(1)}, u32[]{:S(2)}, u32[]{:S(2)}) %collective-permute-start.7) | collective-permute-done | bytes 1048608 | tf_op jit(solution)/shard_map/ppermute | solution.py:409
  57.0 1.8 add_convert_fusion.1
  58.9 2.2 %collective-permute-start.10 = (bf16[128,1024]{1,0:T(8,128)(2,1)S(1)}, bf16[128,1024]{1,0:T(8,128)(2,1)S(1)}, u32[]{:S(2)}, u32[]{:S(2)}) collective-permute-start(bf16[128,1024]{1,0:T(8,128)(2,1)S(1)} %get-tuple-element.81), channel_id=1, source_target_pairs={{0,6},{1,7},{2,0},{3,1},{4,2},{5,3},{6,4},{7,5},{8,14},{9,15},{10,... | collective-permute-start | bytes 786440 | tf_op jit(solution)/shard_map/ppermute | solution.py:413
  62.6 10.2 %collective-permute-done.10.y3 = bf16[128,1024]{1,0:T(8,128)(2,1)S(1)} collective-permute-done((bf16[128,1024]{1,0:T(8,128)(2,1)S(1)}, bf16[128,1024]{1,0:T(8,128)(2,1)S(1)}, u32[]{:S(2)}, u32[]{:S(2)}) %collective-permute-start.10) | collective-permute-done | bytes 262176 | tf_op jit(solution)/shard_map/ppermute | solution.py:413
  72.8 3.7 %collective-permute-done.8.y1 = bf16[128,1024]{1,0:T(8,128)(2,1)S(1)} collective-permute-done((bf16[128,1024]{1,0:T(8,128)(2,1)S(1)}, bf16[128,1024]{1,0:T(8,128)(2,1)S(1)}, u32[]{:S(2)}, u32[]{:S(2)}) %collective-permute-start.8) | collective-permute-done | bytes 262176 | tf_op jit(solution)/shard_map/ppermute | solution.py:413
  76.5 1.8 atom_update.1
  78.3 2.1 collective-permute-start.12
  80.4 1.7 collective-permute-start.11
  82.1 11.3 %collective-permute-done.13.refs_3_ = bf16[128,1024]{1,0:T(8,128)(2,1)S(1)} collective-permute-done((bf16[128,1024]{1,0:T(8,128)(2,1)S(1)}, bf16[128,1024]{1,0:T(8,128)(2,1)S(1)}, u32[]{:S(2)}, u32[]{:S(2)}) %collective-permute-start.13) | collective-permute-done | bytes 262176 | tf_op jit(solution)/shard_map/ppermute | solution.py:413
  95.7 6.6 %edge_backward.1 = (bf16[1024,1024]{1,0:T(8,128)(2,1)}, bf16[64,16,1024]{2,1,0:T(8,128)(2,1)S(1)}, bf16[64,16,1024]{2,1,0:T(8,128)(2,1)S(1)}) custom-call(bf16[128,1024]{1,0:T(8,128)(2,1)S(1)} %get-tuple-element.53.refs_0_, bf16[128,1024]{1,0:T(8,128)(2,1)S(1)} %collective-permute-done.11.refs_1_, bf16[128,1024]{1,0:T(8,128)(2,1)S(1)} %collective-permute-done.12.refs_2_, ...), custom_call_target="tpu_custom_call" | custom-call | flops 4729999872 | bytes 12582912 | tf_op jit(solution)/shard_map/edge_backward/pallas_call | solution.py:251
  104.1 2.7 %project_back.1.refs_1_ = bf16[1024,1024]{1,0:T(8,128)(2,1)S(1)} custom-call(bf16[1024,1024]{1,0:T(8,128)(2,1)S(1)} %copy-done.6, bf16[1024,1024]{1,0:T(8,128)(2,1)S(1)} %copy-done.5), custom_call_target="tpu_custom_call" | custom-call | flops 2150000128 | bytes 6291456 | tf_op jit(solution)/shard_map/project_back/pallas_call | solution.py:369
  108.2 2.3 %add.51 = bf16[64,16,1024]{2,1,0:T(8,128)(2,1)} add(bf16[64,16,1024]{2,1,0:T(8,128)(2,1)S(1)} %get-tuple-element.58, bf16[64,16,1024]{2,1,0:T(8,128)(2,1)S(1)} %collective-permute-done.18) | non-fusion elementwise | flops 1048576 | bytes 6291456 | tf_op jit(solution)/shard_map/add | solution.py:433
  110.6 10.2 %all-to-all-start = ((bf16[64,16,1024]{2,1,0:T(8,128)(2,1)}), bf16[64,16,1024]{2,1,0:T(8,128)(2,1)S(1)}, u32[]{:S(2)}, u32[]{:S(2)}) async-start(bf16[64,16,1024]{2,1,0:T(8,128)(2,1)} %add.51), calls=%async_computation | async-start | bytes 4194304 | tf_op jit(solution)/shard_map/all_to_all | solution.py:438
  120.8 28.5 %trip_backward.1 = (bf16[2048,1024]{1,0:T(8,128)(2,1)}, bf16[64,16,1152]{2,1,0:T(8,128)(2,1)}, bf16[64,16,1152]{2,1,0:T(8,128)(2,1)}) custom-call(s32[1]{0:T(128)} %bitcast.7.refs_8_.refs_0_, bf16[1024,1024]{1,0:T(8,128)(2,1)} %copy-done.7, bf16[2048,1024]{1,0:T(8,128)(2,1)} %get-tuple-element.61.refs_2_, bf16[1024,1024]{1,0:T(8,128)(2,1)} %get-tuple-element.62.refs_3_, ...), custom_call_target="tpu_custom_call" | custom-call | flops 18489999360 | bytes 25165824 | tf_op jit(solution)/shard_map/trip_backward/pallas_call | solution.py:326
  149.3 1.6 all-to-all-done
  151.3 4.4 %collective-permute-done.19 = bf16[64,16,1152]{2,1,0:T(8,128)(2,1)S(1)} collective-permute-done((bf16[64,16,1152]{2,1,0:T(8,128)(2,1)}, bf16[64,16,1152]{2,1,0:T(8,128)(2,1)S(1)}, u32[]{:S(2)}, u32[]{:S(2)}) %collective-permute-start.19) | collective-permute-done | bytes 2359328 | tf_op jit(solution)/shard_map/ppermute | solution.py:409
  155.7 3.7 %add.52 = bf16[64,16,1152]{2,1,0:T(8,128)(2,1)} add(bf16[64,16,1152]{2,1,0:T(8,128)(2,1)} %get-tuple-element.70, bf16[64,16,1152]{2,1,0:T(8,128)(2,1)S(1)} %collective-permute-done.19) | non-fusion elementwise | flops 1179648 | bytes 7077888 | tf_op jit(solution)/shard_map/add | solution.py:433
  159.3 5.8 %all-to-all-start.1 = ((bf16[64,16,1152]{2,1,0:T(8,128)(2,1)}), bf16[64,16,1152]{2,1,0:T(8,128)(2,1)S(1)}, u32[]{:S(2)}, u32[]{:S(2)}) async-start(bf16[64,16,1152]{2,1,0:T(8,128)(2,1)} %add.52), calls=%async_computation.1 | async-start | bytes 4718592 | tf_op jit(solution)/shard_map/all_to_all | solution.py:446
  165.1 8.5 %atom_backward.1 = (bf16[512,1024]{1,0:T(8,128)(2,1)}, bf16[512,1024]{1,0:T(8,128)(2,1)}) custom-call(bf16[2048,1024]{1,0:T(8,128)(2,1)} %get-tuple-element.73.sums, bf16[2048,1024]{1,0:T(8,128)(2,1)} %w_dst.1, bf16[2048,1024]{1,0:T(8,128)(2,1)} %w_dst.1), custom_call_target="tpu_custom_call" | custom-call | flops 4300000256 | bytes 10485760 | tf_op jit(solution)/shard_map/atom_backward/pallas_call | solution.py:390
  173.6 2.9 %collective-permute-done.20 = bf16[512,1024]{1,0:T(8,128)(2,1)S(1)} collective-permute-done((bf16[512,1024]{1,0:T(8,128)(2,1)}, bf16[512,1024]{1,0:T(8,128)(2,1)S(1)}, u32[]{:S(2)}, u32[]{:S(2)}) %collective-permute-start.20) | collective-permute-done | bytes 1048608 | tf_op jit(solution)/shard_map/ppermute | solution.py:409
  176.5 1.6 add_convert_fusion
  180.6 1.8 collective-permute-start.23
  182.3 1.8 collective-permute-start.22
  184.7 14.1 %all-to-all-done.1 = bf16[64,16,1152]{2,1,0:T(8,128)(2,1)S(1)} async-done(((bf16[64,16,1152]{2,1,0:T(8,128)(2,1)}), bf16[64,16,1152]{2,1,0:T(8,128)(2,1)S(1)}, u32[]{:S(2)}, u32[]{:S(2)}) %all-to-all-start.1) | async-done | bytes 2359328 | tf_op jit(solution)/shard_map/all_to_all | solution.py:446
  199.9 4.2 %all-to-all-start.2 = ((bf16[4,16,1152]{2,1,0:T(8,128)(2,1)}), bf16[4,16,1152]{2,1,0:T(8,128)(2,1)S(1)}, u32[]{:S(2)}, u32[]{:S(2)}) async-start(bf16[4,16,1152]{2,1,0:T(8,128)(2,1)} %reduce_sum.31), calls=%async_computation.2 | async-start | bytes 294912 | tf_op jit(solution)/shard_map/all_to_all | solution.py:455
  204.1 2.0 fusion
  206.1 4.1 %all-to-all-done.2 = bf16[4,16,1152]{2,1,0:T(8,128)(2,1)S(1)} async-done(((bf16[4,16,1152]{2,1,0:T(8,128)(2,1)}), bf16[4,16,1152]{2,1,0:T(8,128)(2,1)S(1)}, u32[]{:S(2)}, u32[]{:S(2)}) %all-to-all-start.2) | async-done | bytes 147488 | tf_op jit(solution)/shard_map/all_to_all | solution.py:455
  (84 shorter events, 17.5 us)
Async XLA Ops:
  0.6 11.6 %collective-permute-start.2 = (bf16[128,1024]{1,0:T(8,128)(2,1)}, bf16[128,1024]{1,0:T(8,128)(2,1)S(1)}, u32[]{:S(2)}, u32[]{:S(2)}) collective-permute-start(bf16[128,1024]{1,0:T(8,128)(2,1)} %bitcast.17), channel_id=1, source_target_pairs={{0,2},{1,3},{2,4},{3,5},{4,6},{5,7},{6,0},{7,1},{8,10},{9,11},{10,... | collective-permute-start | bytes 786440 | tf_op jit(solution)/shard_map/ppermute | solution.py:413
  2.7 15.4 %collective-permute-start.1 = (bf16[128,1024]{1,0:T(8,128)(2,1)}, bf16[128,1024]{1,0:T(8,128)(2,1)S(1)}, u32[]{:S(2)}, u32[]{:S(2)}) collective-permute-start(bf16[128,1024]{1,0:T(8,128)(2,1)} %bitcast.18), channel_id=1, source_target_pairs={{0,4},{1,5},{2,6},{3,7},{4,0},{5,1},{6,2},{7,3},{8,12},{9,13},{10,... | collective-permute-start | bytes 786440 | tf_op jit(solution)/shard_map/ppermute | solution.py:413
  6.3 11.9 %collective-permute-start = (bf16[128,1024]{1,0:T(8,128)(2,1)}, bf16[128,1024]{1,0:T(8,128)(2,1)S(1)}, u32[]{:S(2)}, u32[]{:S(2)}) collective-permute-start(bf16[128,1024]{1,0:T(8,128)(2,1)} %bitcast.19), channel_id=1, source_target_pairs={{0,6},{1,7},{2,0},{3,1},{4,2},{5,3},{6,4},{7,5},{8,14},{9,15},{10,... | collective-permute-start | bytes 786440 | tf_op jit(solution)/shard_map/ppermute | solution.py:413
  7.3 12.8 %collective-permute-start.3 = (bf16[128,1024]{1,0:T(8,128)(2,1)}, bf16[128,1024]{1,0:T(8,128)(2,1)S(1)}, u32[]{:S(2)}, u32[]{:S(2)}) collective-permute-start(bf16[128,1024]{1,0:T(8,128)(2,1)} %bitcast.20), channel_id=1, source_target_pairs={{0,1},{1,0},{2,3},{3,2},{4,5},{5,4},{6,7},{7,6},{8,9},{9,8},{10,11... | collective-permute-start | bytes 786440 | tf_op jit(solution)/shard_map/ppermute | solution.py:409
  18.1 2.0 collective-permute-start.4
  18.2 1.9 collective-permute-start.5
  18.7 1.8 collective-permute-start.6
  53.8 3.2 %collective-permute-start.7 = (bf16[512,1024]{1,0:T(8,128)(2,1)}, bf16[512,1024]{1,0:T(8,128)(2,1)S(1)}, u32[]{:S(2)}, u32[]{:S(2)}) collective-permute-start(bf16[512,1024]{1,0:T(8,128)(2,1)} %get-tuple-element.50), channel_id=1, source_target_pairs={{0,1},{1,0},{2,3},{3,2},{4,5},{5,4},{6,7},{7,6},{8,9},{9,8},{10,11... | collective-permute-start | bytes 3145736 | tf_op jit(solution)/shard_map/ppermute | solution.py:409
  57.0 19.5 %copy-start.1 = (bf16[1,128,1024]{2,1,0:T(8,128)(2,1)S(1)}, bf16[1,128,1024]{2,1,0:T(8,128)(2,1)}, u32[]{:S(2)}) copy-start(bf16[1,128,1024]{2,1,0:T(8,128)(2,1)} %param.26) | copy-start | bytes 786436
  57.0 19.5 %copy-start.2 = (bf16[1,128,1024]{2,1,0:T(8,128)(2,1)S(1)}, bf16[1,128,1024]{2,1,0:T(8,128)(2,1)}, u32[]{:S(2)}) copy-start(bf16[1,128,1024]{2,1,0:T(8,128)(2,1)} %param.14) | copy-start | bytes 786436
  58.8 36.8 %copy-start.8 = (bf16[1024,1024]{1,0:T(8,128)(2,1)S(1)}, bf16[1024,1024]{1,0:T(8,128)(2,1)}, u32[]{:S(2)}) copy-start(bf16[1024,1024]{1,0:T(8,128)(2,1)} %get-tuple-element.54.refs_11_) | copy-start | bytes 6291460
  58.9 36.7 %copy-start.3 = (s32[1,1024]{1,0:T(1,128)S(1)}, s32[1,1024]{1,0:T(1,128)}, u32[]{:S(2)}) copy-start(s32[1,1024]{1,0:T(1,128)} %get-tuple-element.87.refs_9_.refs_10_) | copy-start | bytes 12292
  58.9 36.7 %copy-start.4 = (bf16[1,1024,1024]{2,1,0:T(8,128)(2,1)S(1)}, bf16[1,1024,1024]{2,1,0:T(8,128)(2,1)}, u32[]{:S(2)}) copy-start(bf16[1,1024,1024]{2,1,0:T(8,128)(2,1)} %param.27) | copy-start | bytes 6291460
  58.9 13.9 %collective-permute-start.10 = (bf16[128,1024]{1,0:T(8,128)(2,1)S(1)}, bf16[128,1024]{1,0:T(8,128)(2,1)S(1)}, u32[]{:S(2)}, u32[]{:S(2)}) collective-permute-start(bf16[128,1024]{1,0:T(8,128)(2,1)S(1)} %get-tuple-element.81), channel_id=1, source_target_pairs={{0,6},{1,7},{2,0},{3,1},{4,2},{5,3},{6,4},{7,5},{8,14},{9,15},{10,... | collective-permute-start | bytes 786440 | tf_op jit(solution)/shard_map/ppermute | solution.py:413
  61.1 11.7 %collective-permute-start.9 = (bf16[128,1024]{1,0:T(8,128)(2,1)S(1)}, bf16[128,1024]{1,0:T(8,128)(2,1)S(1)}, u32[]{:S(2)}, u32[]{:S(2)}) collective-permute-start(bf16[128,1024]{1,0:T(8,128)(2,1)S(1)} %get-tuple-element.82), channel_id=1, source_target_pairs={{0,4},{1,5},{2,6},{3,7},{4,0},{5,1},{6,2},{7,3},{8,12},{9,13},{10,... | collective-permute-start | bytes 786440 | tf_op jit(solution)/shard_map/ppermute | solution.py:413
  62.2 14.3 %collective-permute-start.8 = (bf16[128,1024]{1,0:T(8,128)(2,1)S(1)}, bf16[128,1024]{1,0:T(8,128)(2,1)S(1)}, u32[]{:S(2)}, u32[]{:S(2)}) collective-permute-start(bf16[128,1024]{1,0:T(8,128)(2,1)S(1)} %get-tuple-element.83), channel_id=1, source_target_pairs={{0,2},{1,3},{2,4},{3,5},{4,6},{5,7},{6,0},{7,1},{8,10},{9,11},{10,... | collective-permute-start | bytes 786440 | tf_op jit(solution)/shard_map/ppermute | solution.py:413
  78.3 15.1 %collective-permute-start.13 = (bf16[128,1024]{1,0:T(8,128)(2,1)S(1)}, bf16[128,1024]{1,0:T(8,128)(2,1)S(1)}, u32[]{:S(2)}, u32[]{:S(2)}) collective-permute-start(bf16[128,1024]{1,0:T(8,128)(2,1)S(1)} %get-tuple-element.53.refs_0_), channel_id=1, source_target_pairs={{0,2},{1,3},{2,4},{3,5},{4,6},{5,7},{6,0},{7,1},{8,10},{9,11},{10,... | collective-permute-start | bytes 786440 | tf_op jit(solution)/shard_map/ppermute | solution.py:413
  78.3 15.1 %collective-permute-start.12 = (bf16[128,1024]{1,0:T(8,128)(2,1)S(1)}, bf16[128,1024]{1,0:T(8,128)(2,1)S(1)}, u32[]{:S(2)}, u32[]{:S(2)}) collective-permute-start(bf16[128,1024]{1,0:T(8,128)(2,1)S(1)} %get-tuple-element.53.refs_0_), channel_id=1, source_target_pairs={{0,4},{1,5},{2,6},{3,7},{4,0},{5,1},{6,2},{7,3},{8,12},{9,13},{10,... | collective-permute-start | bytes 786440 | tf_op jit(solution)/shard_map/ppermute | solution.py:413
  80.4 13.6 %collective-permute-start.11 = (bf16[128,1024]{1,0:T(8,128)(2,1)S(1)}, bf16[128,1024]{1,0:T(8,128)(2,1)S(1)}, u32[]{:S(2)}, u32[]{:S(2)}) collective-permute-start(bf16[128,1024]{1,0:T(8,128)(2,1)S(1)} %get-tuple-element.53.refs_0_), channel_id=1, source_target_pairs={{0,6},{1,7},{2,0},{3,1},{4,2},{5,3},{6,4},{7,5},{8,14},{9,15},{10,... | collective-permute-start | bytes 786440 | tf_op jit(solution)/shard_map/ppermute | solution.py:413
  82.1 11.9 %collective-permute-start.14 = (bf16[128,1024]{1,0:T(8,128)(2,1)S(1)}, bf16[128,1024]{1,0:T(8,128)(2,1)S(1)}, u32[]{:S(2)}, u32[]{:S(2)}) collective-permute-start(bf16[128,1024]{1,0:T(8,128)(2,1)S(1)} %get-tuple-element.53.refs_0_), channel_id=1, source_target_pairs={{0,1},{1,0},{2,3},{3,2},{4,5},{5,4},{6,7},{7,6},{8,9},{9,8},{10,11... | collective-permute-start | bytes 786440 | tf_op jit(solution)/shard_map/ppermute | solution.py:409
  93.4 1.5 collective-permute-start.17
  93.4 1.9 collective-permute-start.16
  94.0 1.7 collective-permute-start.15
  102.3 5.9 %collective-permute-start.18 = (bf16[64,16,1024]{2,1,0:T(8,128)(2,1)S(1)}, bf16[64,16,1024]{2,1,0:T(8,128)(2,1)S(1)}, u32[]{:S(2)}, u32[]{:S(2)}) collective-permute-start(bf16[64,16,1024]{2,1,0:T(8,128)(2,1)S(1)} %get-tuple-element.59), channel_id=1, source_target_pairs={{0,1},{1,0},{2,3},{3,2},{4,5},{5,4},{6,7},{7,6},{8,9},{9,8},{10,11... | collective-permute-start | bytes 6291464 | tf_op jit(solution)/shard_map/ppermute | solution.py:409
  110.6 40.4 %all-to-all-start = ((bf16[64,16,1024]{2,1,0:T(8,128)(2,1)}), bf16[64,16,1024]{2,1,0:T(8,128)(2,1)S(1)}, u32[]{:S(2)}, u32[]{:S(2)}) async-start(bf16[64,16,1024]{2,1,0:T(8,128)(2,1)} %add.51), calls=%async_computation | async-start | bytes 4194304 | tf_op jit(solution)/shard_map/all_to_all | solution.py:438
  150.9 4.7 %collective-permute-start.19 = (bf16[64,16,1152]{2,1,0:T(8,128)(2,1)}, bf16[64,16,1152]{2,1,0:T(8,128)(2,1)S(1)}, u32[]{:S(2)}, u32[]{:S(2)}) collective-permute-start(bf16[64,16,1152]{2,1,0:T(8,128)(2,1)} %get-tuple-element.71), channel_id=1, source_target_pairs={{0,1},{1,0},{2,3},{3,2},{4,5},{5,4},{6,7},{7,6},{8,9},{9,8},{10,11... | collective-permute-start | bytes 7077896 | tf_op jit(solution)/shard_map/ppermute | solution.py:409
  159.3 39.5 %all-to-all-start.1 = ((bf16[64,16,1152]{2,1,0:T(8,128)(2,1)}), bf16[64,16,1152]{2,1,0:T(8,128)(2,1)S(1)}, u32[]{:S(2)}, u32[]{:S(2)}) async-start(bf16[64,16,1152]{2,1,0:T(8,128)(2,1)} %add.52), calls=%async_computation.1 | async-start | bytes 4718592 | tf_op jit(solution)/shard_map/all_to_all | solution.py:446
  173.6 2.9 %collective-permute-start.20 = (bf16[512,1024]{1,0:T(8,128)(2,1)}, bf16[512,1024]{1,0:T(8,128)(2,1)S(1)}, u32[]{:S(2)}, u32[]{:S(2)}) collective-permute-start(bf16[512,1024]{1,0:T(8,128)(2,1)} %get-tuple-element.75), channel_id=1, source_target_pairs={{0,1},{1,0},{2,3},{3,2},{4,5},{5,4},{6,7},{7,6},{8,9},{9,8},{10,11... | collective-permute-start | bytes 3145736 | tf_op jit(solution)/shard_map/ppermute | solution.py:409
  179.1 25.0 %collective-permute-start.21 = (bf16[128,1024]{1,0:T(8,128)(2,1)}, bf16[128,1024]{1,0:T(8,128)(2,1)S(1)}, u32[]{:S(2)}, u32[]{:S(2)}) collective-permute-start(bf16[128,1024]{1,0:T(8,128)(2,1)} %get-tuple-element.78), channel_id=1, source_target_pairs={{0,2},{1,3},{2,4},{3,5},{4,6},{5,7},{6,0},{7,1},{8,10},{9,11},{10,... | collective-permute-start | bytes 786440 | tf_op jit(solution)/shard_map/ppermute | solution.py:413
  180.6 23.6 %collective-permute-start.23 = (bf16[128,1024]{1,0:T(8,128)(2,1)}, bf16[128,1024]{1,0:T(8,128)(2,1)S(1)}, u32[]{:S(2)}, u32[]{:S(2)}) collective-permute-start(bf16[128,1024]{1,0:T(8,128)(2,1)} %get-tuple-element.79), channel_id=1, source_target_pairs={{0,6},{1,7},{2,0},{3,1},{4,2},{5,3},{6,4},{7,5},{8,14},{9,15},{10,... | collective-permute-start | bytes 786440 | tf_op jit(solution)/shard_map/ppermute | solution.py:413
  182.3 21.8 %collective-permute-start.22 = (bf16[128,1024]{1,0:T(8,128)(2,1)S(1)}, bf16[128,1024]{1,0:T(8,128)(2,1)}, u32[]{:S(2)}, u32[]{:S(2)}) collective-permute-start(bf16[128,1024]{1,0:T(8,128)(2,1)S(1)} %get-tuple-element.80), channel_id=1, source_target_pairs={{0,4},{1,5},{2,6},{3,7},{4,0},{5,1},{6,2},{7,3},{8,12},{9,13},{10,... | collective-permute-start | bytes 786440 | tf_op jit(solution)/shard_map/ppermute | solution.py:413
  199.9 10.3 %all-to-all-start.2 = ((bf16[4,16,1152]{2,1,0:T(8,128)(2,1)}), bf16[4,16,1152]{2,1,0:T(8,128)(2,1)S(1)}, u32[]{:S(2)}, u32[]{:S(2)}) async-start(bf16[4,16,1152]{2,1,0:T(8,128)(2,1)} %reduce_sum.31), calls=%async_computation.2 | async-start | bytes 294912 | tf_op jit(solution)/shard_map/all_to_all | solution.py:455
  (15 other events, 85.3 us)

commit v2 on v0

--- a/solution.py
+++ b/solution.py
@@ -273,9 +273,9 @@
 
 
 def trip_body(*refs):
-    core, d_summed, in_rows, slope, turned, filters, rows, tin, ttg = refs[:9]
-    d_preact, keep, give = refs[9:12]
-    gather_tgt, scatter_in, msg, d_filter, held, grad_basis, folded = refs[12:]
+    core, d_edge, w_out, in_rows, slope, turned, filters, rows, tin, ttg = refs[:10]
+    d_preact, keep, give = refs[10:13]
+    gather_tgt, scatter_in, msg, d_filter, held, grad_basis, folded = refs[13:]
     step = pl.program_id(0)
 
     @pl.when(step == 0)
@@ -285,9 +285,10 @@
 
     @pl.when(step < STEPS)
     def _():
+        d_summed = dot_nt(d_edge[...], w_out[...]).astype(BF)
         for t in range(2):
             part = slice(t * 1024, (t + 1) * 1024)
-            d_trip = dot_nn(gather_tgt[part, :], d_summed[...]).astype(BF)
+            d_trip = dot_nn(gather_tgt[part, :], d_summed).astype(BF)
             d_filter[part, :] = d_trip * in_rows[part, :]
             msg[part, :] = d_trip * filters[part, :]
         at = pl.ds(pl.multiple_of(step * COL, COL), COL)
@@ -318,14 +319,15 @@
     give[...] = jnp.where(core == 0, odd, even)
 
 
-def trip_backward(core, d_summed, in_rows, slope, turned, filters, rows, tin, ttg):
+def trip_backward(core, d_edge, w_out, in_rows, slope, turned, filters, rows, tin, ttg):
     chunks = pl.BlockSpec((64 // STEPS, 16, CHUNK), lambda j: (jnp.maximum(j - STEPS, 0), 0, 0))
     return call(
         trip_body,
         (2 * STEPS,),
         [
             SCALAR,
-            early(1024),
+            full((1024, 1024)),
+            pl.BlockSpec((COL, 1024), lambda j: (jnp.minimum(j, STEPS - 1), 0)),
             early(2048),
             early(1024),
             full((128, 2048)),
@@ -349,30 +351,11 @@
             pltpu.VMEM((128, 1024), F32),
             pltpu.VMEM((1024, 128), F32),
         ],
-        int(2.15e9 * 6.6),
+        int(2.15e9 * 7.6),
         24 << 20,
         60,
         "trip_backward",
-    )(core, d_summed, in_rows, slope, turned, filters, rows, tin, ttg)
-
-
-def project_body(d_edge, w_out, d_summed):
-    d_summed[...] = dot_nt(d_edge[...], w_out[...]).astype(BF)
-
-
-def project_back(d_edge, w_out):
-    return call(
-        project_body,
-        (STEPS,),
-        [full((1024, 1024)), pl.BlockSpec((COL, 1024), lambda j: (j, 0))],
-        cols(1024),
-        jax.ShapeDtypeStruct((1024, 1024), BF),
-        [],
-        int(2.15e9),
-        6 << 20,
-        24,
-        "project_back",
-    )(d_edge, w_out)
+    )(core, d_edge, w_out, in_rows, slope, turned, filters, rows, tin, ttg)
 
 
 def atom_sums_body(d_preact, src, dst, sums, scatter):
@@ -459,6 +442,20 @@
 
 def add_chunks(spread):
     return jnp.sum(spread.astype(F32), axis=0)
+
+
+def spread_plane(both):
+    return lax.all_to_all(both, "dp", 0, 0, tiled=True)
+
+
+def add_plane(spread):
+    return jnp.sum(spread.reshape(16, 4, 16, -1).astype(F32), axis=0).astype(BF)
+
+
+def add_line(plane):
+    groups = [[2 * z + c for z in range(4)] for c in range(2)]
+    last = lax.all_to_all(plane, "graph", 0, 0, tiled=True, axis_index_groups=groups)
+    return jnp.sum(last.astype(F32), axis=0)
 
 
 def tie(*values):
@@ -505,20 +502,19 @@
     d_edge, keep, give = edge_backward(
         gather_graph(d_sum)[0], core[None], dst, edge_cotan[0], summed, atom_sum, d_z
     )
-    both = add_core(keep, give)
-    d_summed, both = tie(project_back(d_edge, w_out), both)
+    d_edge, both = tie(d_edge, add_core(keep, give))
     spread = spread_chunks(both)
     d_preact, keep, give = trip_backward(
-        core[None], d_summed, in_rows, slope, turned, filters, rows, tin, ttg
+        core[None], d_edge, w_out, in_rows, slope, turned, filters, rows, tin, ttg
     )
     d_preact, spread, keep, give = tie(d_preact, spread, keep, give)
     out_atom = add_chunks(spread)
     both = add_core(keep, give)
-    sums, both, out_atom = tie(atom_sums(d_preact, src, dst), both, out_atom)
-    spread = spread_chunks(both)
-    back = scatter_graph(*atom_backward(sums, w_pair))
+    d_preact, both, out_atom = tie(d_preact, both, out_atom)
+    spread = spread_plane(both)
+    back = scatter_graph(*atom_backward(atom_sums(d_preact, src, dst), w_pair))
     grads_new = (cotan.astype(F32) + sum(b.astype(F32) for b in back)).astype(BF)
-    pair = add_chunks(spread)
+    pair = add_line(add_plane(spread))
     pair_total, basis_total = pair[:, :1024], pair[:8, 1024:].reshape(1, 1024)
     out_total, atom_w_total = out_atom[:8], out_atom[8:]
     return (

time: 217 us -> 213 us (0.982)
  the two profiles are of different devices: /device:TPU:1 before, /device:TPU:0 now
where the time goes in v2:
time: 213 us; the launch traced here: 210 us
  Pallas kernels  82.5 us (39%)
  waiting for transfers between devices  70.3 us (33%)
  starting transfers between devices  38.6 us (18%)
  other arithmetic  13.6 us (6%)
  local copies, waits for them, and re-layouts  2.77 us (1%)
    pallas_call x1, Pallas kernels, forward(): call(forward_body, (2 * STEPS,), [full((128, 1024))] * 8 + [full((1, 1024...  32.8 us
    ppermute x12, waiting for transfers between devices, along_z(): lax.ppermute(x, 'graph', [(2 * z + c, 2 * ((z + shift) % 4) + c) for z in...  31.1 us
    pallas_call x1, Pallas kernels, trip_backward(): call(trip_body, (2 * STEPS,), [SCALAR, full((1024, 1024)), pl.BlockSpec((...  26.1 us
    ppermute x12, starting transfers between devices, along_z(): lax.ppermute(x, 'graph', [(2 * z + c, 2 * ((z + shift) % 4) + c) for z in...  18.1 us
    ppermute x12, waiting for transfers between devices, swap_core(): return lax.ppermute(x, 'graph', [(i, i ^ 1) for i in range(8)])  15.5 us
    all_to_all x1, waiting for transfers between devices, spread_plane(): return lax.all_to_all(both, 'dp', 0, 0, tiled=True)  14.8 us
    all_to_all x1, starting transfers between devices, spread_chunks(): lax.all_to_all(both, ('dp', 'graph'), 0, 0, tiled=True, axis_index_groups...  10.1 us
    pallas_call x1, Pallas kernels, edge_backward(): call(back_edge_body, (STEPS,), [cols(128)] * 8 + [SCALAR, full((1, 1024))...  6.61 us
  transfers between devices with their start and end apart: 27, of which 16 were waited for; matrix products, arithmetic and copies ran while one was open for 3% of the time, Pallas kernels for 20%

profile of v2, /device:TPU:0, one launch (start us, length us, event | category | flops | bytes accessed | tf_op | source)
XLA Modules:
  0.0 209.6 jit_solution(1875683472348783469)
XLA Ops:
  0.6 2.1 collective-permute-start.2
  2.7 3.6 %collective-permute-start.1 = (bf16[128,1024]{1,0:T(8,128)(2,1)}, bf16[128,1024]{1,0:T(8,128)(2,1)S(1)}, u32[]{:S(2)}, u32[]{:S(2)}) collective-permute-start(bf16[128,1024]{1,0:T(8,128)(2,1)} %bitcast.18), channel_id=1, source_target_pairs={{0,4},{1,5},{2,6},{3,7},{4,0},{5,1},{6,2},{7,3},{8,12},{9,13},{10,... | collective-permute-start | bytes 786440 | tf_op jit(solution)/shard_map/ppermute | solution.py:415
  8.0 4.3 %prepare.1 = (bf16[2048,1024]{1,0:T(8,128)(2,1)}, bf16[128,2048]{1,0:T(8,128)(2,1)}) custom-call(bf16[2048,128]{1,0:T(8,128)(2,1)} %bitcast.26, bf16[128,1024]{1,0:T(8,128)(2,1)} %w_basis.1), custom_call_target="tpu_custom_call" | custom-call | flops 1290000000 | bytes 6291456 | tf_op jit(solution)/shard_map/prepare/pallas_call | solution.py:90
  12.3 5.8 %collective-permute-done.1.refs_2_ = bf16[128,1024]{1,0:T(8,128)(2,1)S(1)} collective-permute-done((bf16[128,1024]{1,0:T(8,128)(2,1)}, bf16[128,1024]{1,0:T(8,128)(2,1)S(1)}, u32[]{:S(2)}, u32[]{:S(2)}) %collective-permute-start.1) | collective-permute-done | bytes 262176 | tf_op jit(solution)/shard_map/ppermute | solution.py:415
  21.2 32.8 %forward.1 = (bf16[1024,2048]{1,0:T(8,128)(2,1)}, bf16[2048,1024]{1,0:T(8,128)(2,1)}, bf16[1024,1024]{1,0:T(8,128)(2,1)}, bf16[1024,1024]{1,0:T(8,128)(2,1)}, bf...) custom-call(bf16[128,1024]{1,0:T(8,128)(2,1)} %bitcast.21, ...), custom_call_target="tpu_custom_call" | custom-call | flops 22144999424 | bytes 29360128 | tf_op jit(solution)/shard_map/forward/pallas_call | solution.py:158
  54.6 2.6 %collective-permute-done.7 = bf16[512,1024]{1,0:T(8,128)(2,1)S(1)} collective-permute-done((bf16[512,1024]{1,0:T(8,128)(2,1)}, bf16[512,1024]{1,0:T(8,128)(2,1)S(1)}, u32[]{:S(2)}, u32[]{:S(2)}) %collective-permute-start.7) | collective-permute-done | bytes 1048608 | tf_op jit(solution)/shard_map/ppermute | solution.py:411
  57.2 1.8 add_convert_fusion.1
  59.1 2.1 %collective-permute-start.10 = (bf16[128,1024]{1,0:T(8,128)(2,1)S(1)}, bf16[128,1024]{1,0:T(8,128)(2,1)S(1)}, u32[]{:S(2)}, u32[]{:S(2)}) collective-permute-start(bf16[128,1024]{1,0:T(8,128)(2,1)S(1)} %get-tuple-element.81), channel_id=1, source_target_pairs={{0,6},{1,7},{2,0},{3,1},{4,2},{5,3},{6,4},{7,5},{8,14},{9,15},{10,... | collective-permute-start | bytes 786440 | tf_op jit(solution)/shard_map/ppermute | solution.py:415
  61.2 1.1 collective-permute-start.9
  62.7 10.2 %collective-permute-done.10.y3 = bf16[128,1024]{1,0:T(8,128)(2,1)S(1)} collective-permute-done((bf16[128,1024]{1,0:T(8,128)(2,1)S(1)}, bf16[128,1024]{1,0:T(8,128)(2,1)S(1)}, u32[]{:S(2)}, u32[]{:S(2)}) %collective-permute-start.10) | collective-permute-done | bytes 262176 | tf_op jit(solution)/shard_map/ppermute | solution.py:415
  72.9 3.7 %collective-permute-done.8.y1 = bf16[128,1024]{1,0:T(8,128)(2,1)S(1)} collective-permute-done((bf16[128,1024]{1,0:T(8,128)(2,1)S(1)}, bf16[128,1024]{1,0:T(8,128)(2,1)S(1)}, u32[]{:S(2)}, u32[]{:S(2)}) %collective-permute-start.8) | collective-permute-done | bytes 262176 | tf_op jit(solution)/shard_map/ppermute | solution.py:415
  76.6 1.8 atom_update.1
  78.4 2.1 collective-permute-start.12
  80.4 1.7 collective-permute-start.11
  82.1 11.3 %collective-permute-done.13.refs_3_ = bf16[128,1024]{1,0:T(8,128)(2,1)S(1)} collective-permute-done((bf16[128,1024]{1,0:T(8,128)(2,1)S(1)}, bf16[128,1024]{1,0:T(8,128)(2,1)S(1)}, u32[]{:S(2)}, u32[]{:S(2)}) %collective-permute-start.13) | collective-permute-done | bytes 262176 | tf_op jit(solution)/shard_map/ppermute | solution.py:415
  95.7 6.6 %edge_backward.1 = (bf16[1024,1024]{1,0:T(8,128)(2,1)}, bf16[64,16,1024]{2,1,0:T(8,128)(2,1)S(1)}, bf16[64,16,1024]{2,1,0:T(8,128)(2,1)S(1)}) custom-call(bf16[128,1024]{1,0:T(8,128)(2,1)S(1)} %get-tuple-element.53.refs_0_, bf16[128,1024]{1,0:T(8,128)(2,1)S(1)} %collective-permute-done.11.refs_1_, bf16[128,1024]{1,0:T(8,128)(2,1)S(1)} %collective-permute-done.12.refs_2_, ...), custom_call_target="tpu_custom_call" | custom-call | flops 4729999872 | bytes 12582912 | tf_op jit(solution)/shard_map/edge_backward/pallas_call | solution.py:251
  102.6 4.0 %collective-permute-done.18 = bf16[64,16,1024]{2,1,0:T(8,128)(2,1)S(1)} collective-permute-done((bf16[64,16,1024]{2,1,0:T(8,128)(2,1)S(1)}, bf16[64,16,1024]{2,1,0:T(8,128)(2,1)S(1)}, u32[]{:S(2)}, u32[]{:S(2)}) %collective-permute-start.18) | collective-permute-done | bytes 2097184 | tf_op jit(solution)/shard_map/ppermute | solution.py:411
  106.6 2.5 %add.51 = bf16[64,16,1024]{2,1,0:T(8,128)(2,1)} add(bf16[64,16,1024]{2,1,0:T(8,128)(2,1)S(1)} %get-tuple-element.58, bf16[64,16,1024]{2,1,0:T(8,128)(2,1)S(1)} %collective-permute-done.18) | non-fusion elementwise | flops 1048576 | bytes 6291456 | tf_op jit(solution)/shard_map/add | solution.py:435
  109.1 10.1 %all-to-all-start = ((bf16[64,16,1024]{2,1,0:T(8,128)(2,1)}), bf16[64,16,1024]{2,1,0:T(8,128)(2,1)S(1)}, u32[]{:S(2)}, u32[]{:S(2)}) async-start(bf16[64,16,1024]{2,1,0:T(8,128)(2,1)} %add.51), calls=%async_computation | async-start | bytes 4194304 | tf_op jit(solution)/shard_map/all_to_all | solution.py:440
  119.1 26.1 %trip_backward.1 = (bf16[1024,1024]{1,0:T(8,128)(2,1)}, bf16[64,16,1152]{2,1,0:T(8,128)(2,1)}, bf16[64,16,1152]{2,1,0:T(8,128)(2,1)}) custom-call(s32[1]{0:T(128)} %bitcast.7.refs_8_.refs_0_, bf16[1024,1024]{1,0:T(8,128)(2,1)} %get-tuple-element.60.refs_1_, bf16[1024,1024]{1,0:T(8,128)(2,1)} %refs_2_.1, bf16[2048,1024]{1,0:T(8,128)(2,1)} %get-tuple-element.61.refs_3_, ...), custom_call_target="tpu_custom_call" | custom-call | flops 16339999744 | bytes 25165824 | tf_op jit(solution)/shard_map/trip_backward/pallas_call | solution.py:324
  145.2 3.9 %all-to-all-done = bf16[64,16,1024]{2,1,0:T(8,128)(2,1)S(1)} async-done(((bf16[64,16,1024]{2,1,0:T(8,128)(2,1)}), bf16[64,16,1024]{2,1,0:T(8,128)(2,1)S(1)}, u32[]{:S(2)}, u32[]{:S(2)}) %all-to-all-start) | async-done | bytes 2097184 | tf_op jit(solution)/shard_map/all_to_all | solution.py:440
  149.5 4.4 %collective-permute-done.19 = bf16[64,16,1152]{2,1,0:T(8,128)(2,1)S(1)} collective-permute-done((bf16[64,16,1152]{2,1,0:T(8,128)(2,1)}, bf16[64,16,1152]{2,1,0:T(8,128)(2,1)S(1)}, u32[]{:S(2)}, u32[]{:S(2)}) %collective-permute-start.19) | collective-permute-done | bytes 2359328 | tf_op jit(solution)/shard_map/ppermute | solution.py:411
  153.8 3.7 %add.52 = bf16[64,16,1152]{2,1,0:T(8,128)(2,1)} add(bf16[64,16,1152]{2,1,0:T(8,128)(2,1)} %get-tuple-element.70, bf16[64,16,1152]{2,1,0:T(8,128)(2,1)S(1)} %collective-permute-done.19) | non-fusion elementwise | flops 1179648 | bytes 7077888 | tf_op jit(solution)/shard_map/add | solution.py:435
  157.5 4.8 %all-to-all-start.1 = ((bf16[64,16,1152]{2,1,0:T(8,128)(2,1)}), bf16[64,16,1152]{2,1,0:T(8,128)(2,1)}, u32[]{:S(2)}, u32[]{:S(2)}) async-start(bf16[64,16,1152]{2,1,0:T(8,128)(2,1)} %add.52), calls=%async_computation.1 | async-start | bytes 4718592 | tf_op jit(solution)/shard_map/all_to_all | solution.py:448
  162.4 5.9 %atom_sums.1.sums = bf16[2048,1024]{1,0:T(8,128)(2,1)S(1)} custom-call(bf16[1024,1024]{1,0:T(8,128)(2,1)S(1)} %copy-done.7, s32[1,1024]{1,0:T(1,128)S(1)} %copy-done.4, s32[1,1024]{1,0:T(1,128)S(1)} %copy-done.3), custom_call_target="tpu_custom_call" | custom-call | flops 4300000256 | bytes 6291456 | tf_op jit(solution)/shard_map/atom_sums/pallas_call | solution.py:371
  168.4 4.9 %atom_backward.1 = (bf16[512,1024]{1,0:T(8,128)(2,1)S(1)}, bf16[512,1024]{1,0:T(8,128)(2,1)S(1)}) custom-call(bf16[2048,1024]{1,0:T(8,128)(2,1)S(1)} %atom_sums.1.sums, bf16[2048,1024]{1,0:T(8,128)(2,1)S(1)} %copy-done.5, bf16[2048,1024]{1,0:T(8,128)(2,1)S(1)} %copy-done.5), custom_call_target="tpu_custom_call" | custom-call | flops 4300000256 | bytes 10485760 | tf_op jit(solution)/shard_map/atom_backward/pallas_call | solution.py:392
  173.5 2.5 %collective-permute-done.20 = bf16[512,1024]{1,0:T(8,128)(2,1)S(1)} collective-permute-done((bf16[512,1024]{1,0:T(8,128)(2,1)S(1)}, bf16[512,1024]{1,0:T(8,128)(2,1)S(1)}, u32[]{:S(2)}, u32[]{:S(2)}) %collective-permute-start.20) | collective-permute-done | bytes 1048608 | tf_op jit(solution)/shard_map/ppermute | solution.py:411
  177.1 2.7 %collective-permute-start.23 = (bf16[128,1024]{1,0:T(8,128)(2,1)S(1)}, bf16[128,1024]{1,0:T(8,128)(2,1)S(1)}, u32[]{:S(2)}, u32[]{:S(2)}) collective-permute-start(bf16[128,1024]{1,0:T(8,128)(2,1)S(1)} %get-tuple-element.79), channel_id=1, source_target_pairs={{0,6},{1,7},{2,0},{3,1},{4,2},{5,3},{6,4},{7,5},{8,14},{9,15},{10,... | collective-permute-start | bytes 786440 | tf_op jit(solution)/shard_map/ppermute | solution.py:415
  181.2 14.8 %all-to-all-done.1 = bf16[64,16,1152]{2,1,0:T(8,128)(2,1)} async-done(((bf16[64,16,1152]{2,1,0:T(8,128)(2,1)}), bf16[64,16,1152]{2,1,0:T(8,128)(2,1)}, u32[]{:S(2)}, u32[]{:S(2)}) %all-to-all-start.1) | async-done | bytes 2359328 | tf_op jit(solution)/shard_map/all_to_all | solution.py:448
  196.0 2.7 %reduce_sum.31 = bf16[4,16,1152]{2,1,0:T(8,128)(2,1)} reduce(bf16[16,4,16,1152]{3,2,1,0:T(8,128)(2,1)} %bitcast.11, bf16[]{:T(256)} %constant.74.clone.1), dimensions={0}, to_apply=%region_1.2 | reduce | flops 1105920 | bytes 2506754 | tf_op jit(solution)/shard_map/reduce_sum | solution.py:452
  198.6 3.4 %all-to-all-start.2 = ((bf16[4,16,1152]{2,1,0:T(8,128)(2,1)}), bf16[4,16,1152]{2,1,0:T(8,128)(2,1)S(1)}, u32[]{:S(2)}, u32[]{:S(2)}) async-start(bf16[4,16,1152]{2,1,0:T(8,128)(2,1)} %reduce_sum.31), calls=%async_computation.2 | async-start | bytes 294912 | tf_op jit(solution)/shard_map/all_to_all | solution.py:457
  203.0 5.1 %all-to-all-done.2 = bf16[4,16,1152]{2,1,0:T(8,128)(2,1)S(1)} async-done(((bf16[4,16,1152]{2,1,0:T(8,128)(2,1)}), bf16[4,16,1152]{2,1,0:T(8,128)(2,1)S(1)}, u32[]{:S(2)}, u32[]{:S(2)}) %all-to-all-start.2) | async-done | bytes 147488 | tf_op jit(solution)/shard_map/all_to_all | solution.py:457
  (82 shorter events, 12.8 us)
Async XLA Ops:
  0.6 11.7 %collective-permute-start.2 = (bf16[128,1024]{1,0:T(8,128)(2,1)}, bf16[128,1024]{1,0:T(8,128)(2,1)S(1)}, u32[]{:S(2)}, u32[]{:S(2)}) collective-permute-start(bf16[128,1024]{1,0:T(8,128)(2,1)} %bitcast.17), channel_id=1, source_target_pairs={{0,2},{1,3},{2,4},{3,5},{4,6},{5,7},{6,0},{7,1},{8,10},{9,11},{10,... | collective-permute-start | bytes 786440 | tf_op jit(solution)/shard_map/ppermute | solution.py:415
  2.7 15.4 %collective-permute-start.1 = (bf16[128,1024]{1,0:T(8,128)(2,1)}, bf16[128,1024]{1,0:T(8,128)(2,1)S(1)}, u32[]{:S(2)}, u32[]{:S(2)}) collective-permute-start(bf16[128,1024]{1,0:T(8,128)(2,1)} %bitcast.18), channel_id=1, source_target_pairs={{0,4},{1,5},{2,6},{3,7},{4,0},{5,1},{6,2},{7,3},{8,12},{9,13},{10,... | collective-permute-start | bytes 786440 | tf_op jit(solution)/shard_map/ppermute | solution.py:415
  6.3 11.9 %collective-permute-start = (bf16[128,1024]{1,0:T(8,128)(2,1)}, bf16[128,1024]{1,0:T(8,128)(2,1)S(1)}, u32[]{:S(2)}, u32[]{:S(2)}) collective-permute-start(bf16[128,1024]{1,0:T(8,128)(2,1)} %bitcast.19), channel_id=1, source_target_pairs={{0,6},{1,7},{2,0},{3,1},{4,2},{5,3},{6,4},{7,5},{8,14},{9,15},{10,... | collective-permute-start | bytes 786440 | tf_op jit(solution)/shard_map/ppermute | solution.py:415
  7.3 12.8 %collective-permute-start.3 = (bf16[128,1024]{1,0:T(8,128)(2,1)}, bf16[128,1024]{1,0:T(8,128)(2,1)S(1)}, u32[]{:S(2)}, u32[]{:S(2)}) collective-permute-start(bf16[128,1024]{1,0:T(8,128)(2,1)} %bitcast.20), channel_id=1, source_target_pairs={{0,1},{1,0},{2,3},{3,2},{4,5},{5,4},{6,7},{7,6},{8,9},{9,8},{10,11... | collective-permute-start | bytes 786440 | tf_op jit(solution)/shard_map/ppermute | solution.py:411
  18.1 2.0 collective-permute-start.4
  18.2 1.9 collective-permute-start.5
  18.7 1.8 collective-permute-start.6
  54.1 3.1 %collective-permute-start.7 = (bf16[512,1024]{1,0:T(8,128)(2,1)}, bf16[512,1024]{1,0:T(8,128)(2,1)S(1)}, u32[]{:S(2)}, u32[]{:S(2)}) collective-permute-start(bf16[512,1024]{1,0:T(8,128)(2,1)} %get-tuple-element.50), channel_id=1, source_target_pairs={{0,1},{1,0},{2,3},{3,2},{4,5},{5,4},{6,7},{7,6},{8,9},{9,8},{10,11... | collective-permute-start | bytes 3145736 | tf_op jit(solution)/shard_map/ppermute | solution.py:411
  57.2 19.4 %copy-start.1 = (bf16[1,128,1024]{2,1,0:T(8,128)(2,1)S(1)}, bf16[1,128,1024]{2,1,0:T(8,128)(2,1)}, u32[]{:S(2)}) copy-start(bf16[1,128,1024]{2,1,0:T(8,128)(2,1)} %param.26) | copy-start | bytes 786436
  57.2 19.4 %copy-start.2 = (bf16[1,128,1024]{2,1,0:T(8,128)(2,1)S(1)}, bf16[1,128,1024]{2,1,0:T(8,128)(2,1)}, u32[]{:S(2)}) copy-start(bf16[1,128,1024]{2,1,0:T(8,128)(2,1)} %param.14) | copy-start | bytes 786436
  59.0 36.7 %copy-start.8 = (bf16[1024,1024]{1,0:T(8,128)(2,1)S(1)}, bf16[1024,1024]{1,0:T(8,128)(2,1)}, u32[]{:S(2)}) copy-start(bf16[1024,1024]{1,0:T(8,128)(2,1)} %get-tuple-element.54.refs_11_) | copy-start | bytes 6291460
  59.1 36.6 %copy-start.3 = (s32[1,1024]{1,0:T(1,128)S(1)}, s32[1,1024]{1,0:T(1,128)}, u32[]{:S(2)}) copy-start(s32[1,1024]{1,0:T(1,128)} %get-tuple-element.87.refs_9_.dst) | copy-start | bytes 12292
  59.1 36.6 %copy-start.6 = (bf16[1,1024,1024]{2,1,0:T(8,128)(2,1)S(1)}, bf16[1,1024,1024]{2,1,0:T(8,128)(2,1)}, u32[]{:S(2)}) copy-start(bf16[1,1024,1024]{2,1,0:T(8,128)(2,1)} %param.27) | copy-start | bytes 6291460
  59.1 13.8 %collective-permute-start.10 = (bf16[128,1024]{1,0:T(8,128)(2,1)S(1)}, bf16[128,1024]{1,0:T(8,128)(2,1)S(1)}, u32[]{:S(2)}, u32[]{:S(2)}) collective-permute-start(bf16[128,1024]{1,0:T(8,128)(2,1)S(1)} %get-tuple-element.81), channel_id=1, source_target_pairs={{0,6},{1,7},{2,0},{3,1},{4,2},{5,3},{6,4},{7,5},{8,14},{9,15},{10,... | collective-permute-start | bytes 786440 | tf_op jit(solution)/shard_map/ppermute | solution.py:415
  61.2 11.7 %collective-permute-start.9 = (bf16[128,1024]{1,0:T(8,128)(2,1)S(1)}, bf16[128,1024]{1,0:T(8,128)(2,1)S(1)}, u32[]{:S(2)}, u32[]{:S(2)}) collective-permute-start(bf16[128,1024]{1,0:T(8,128)(2,1)S(1)} %get-tuple-element.82), channel_id=1, source_target_pairs={{0,4},{1,5},{2,6},{3,7},{4,0},{5,1},{6,2},{7,3},{8,12},{9,13},{10,... | collective-permute-start | bytes 786440 | tf_op jit(solution)/shard_map/ppermute | solution.py:415
  62.4 14.2 %collective-permute-start.8 = (bf16[128,1024]{1,0:T(8,128)(2,1)S(1)}, bf16[128,1024]{1,0:T(8,128)(2,1)S(1)}, u32[]{:S(2)}, u32[]{:S(2)}) collective-permute-start(bf16[128,1024]{1,0:T(8,128)(2,1)S(1)} %get-tuple-element.83), channel_id=1, source_target_pairs={{0,2},{1,3},{2,4},{3,5},{4,6},{5,7},{6,0},{7,1},{8,10},{9,11},{10,... | collective-permute-start | bytes 786440 | tf_op jit(solution)/shard_map/ppermute | solution.py:415
  78.4 15.1 %collective-permute-start.13 = (bf16[128,1024]{1,0:T(8,128)(2,1)S(1)}, bf16[128,1024]{1,0:T(8,128)(2,1)S(1)}, u32[]{:S(2)}, u32[]{:S(2)}) collective-permute-start(bf16[128,1024]{1,0:T(8,128)(2,1)S(1)} %get-tuple-element.53.refs_0_), channel_id=1, source_target_pairs={{0,2},{1,3},{2,4},{3,5},{4,6},{5,7},{6,0},{7,1},{8,10},{9,11},{10,... | collective-permute-start | bytes 786440 | tf_op jit(solution)/shard_map/ppermute | solution.py:415
  78.4 15.1 %collective-permute-start.12 = (bf16[128,1024]{1,0:T(8,128)(2,1)S(1)}, bf16[128,1024]{1,0:T(8,128)(2,1)S(1)}, u32[]{:S(2)}, u32[]{:S(2)}) collective-permute-start(bf16[128,1024]{1,0:T(8,128)(2,1)S(1)} %get-tuple-element.53.refs_0_), channel_id=1, source_target_pairs={{0,4},{1,5},{2,6},{3,7},{4,0},{5,1},{6,2},{7,3},{8,12},{9,13},{10,... | collective-permute-start | bytes 786440 | tf_op jit(solution)/shard_map/ppermute | solution.py:415
  80.4 13.6 %collective-permute-start.11 = (bf16[128,1024]{1,0:T(8,128)(2,1)S(1)}, bf16[128,1024]{1,0:T(8,128)(2,1)S(1)}, u32[]{:S(2)}, u32[]{:S(2)}) collective-permute-start(bf16[128,1024]{1,0:T(8,128)(2,1)S(1)} %get-tuple-element.53.refs_0_), channel_id=1, source_target_pairs={{0,6},{1,7},{2,0},{3,1},{4,2},{5,3},{6,4},{7,5},{8,14},{9,15},{10,... | collective-permute-start | bytes 786440 | tf_op jit(solution)/shard_map/ppermute | solution.py:415
  82.1 11.9 %collective-permute-start.14 = (bf16[128,1024]{1,0:T(8,128)(2,1)S(1)}, bf16[128,1024]{1,0:T(8,128)(2,1)S(1)}, u32[]{:S(2)}, u32[]{:S(2)}) collective-permute-start(bf16[128,1024]{1,0:T(8,128)(2,1)S(1)} %get-tuple-element.53.refs_0_), channel_id=1, source_target_pairs={{0,1},{1,0},{2,3},{3,2},{4,5},{5,4},{6,7},{7,6},{8,9},{9,8},{10,11... | collective-permute-start | bytes 786440 | tf_op jit(solution)/shard_map/ppermute | solution.py:411
  93.4 1.5 collective-permute-start.17
  93.4 1.9 collective-permute-start.16
  94.1 1.7 collective-permute-start.15
  102.3 4.2 %collective-permute-start.18 = (bf16[64,16,1024]{2,1,0:T(8,128)(2,1)S(1)}, bf16[64,16,1024]{2,1,0:T(8,128)(2,1)S(1)}, u32[]{:S(2)}, u32[]{:S(2)}) collective-permute-start(bf16[64,16,1024]{2,1,0:T(8,128)(2,1)S(1)} %get-tuple-element.59), channel_id=1, source_target_pairs={{0,1},{1,0},{2,3},{3,2},{4,5},{5,4},{6,7},{7,6},{8,9},{9,8},{10,11... | collective-permute-start | bytes 6291464 | tf_op jit(solution)/shard_map/ppermute | solution.py:411
  109.1 40.0 %all-to-all-start = ((bf16[64,16,1024]{2,1,0:T(8,128)(2,1)}), bf16[64,16,1024]{2,1,0:T(8,128)(2,1)S(1)}, u32[]{:S(2)}, u32[]{:S(2)}) async-start(bf16[64,16,1024]{2,1,0:T(8,128)(2,1)} %add.51), calls=%async_computation | async-start | bytes 4194304 | tf_op jit(solution)/shard_map/all_to_all | solution.py:440
  149.1 4.7 %collective-permute-start.19 = (bf16[64,16,1152]{2,1,0:T(8,128)(2,1)}, bf16[64,16,1152]{2,1,0:T(8,128)(2,1)S(1)}, u32[]{:S(2)}, u32[]{:S(2)}) collective-permute-start(bf16[64,16,1152]{2,1,0:T(8,128)(2,1)} %get-tuple-element.71), channel_id=1, source_target_pairs={{0,1},{1,0},{2,3},{3,2},{4,5},{5,4},{6,7},{7,6},{8,9},{9,8},{10,11... | collective-permute-start | bytes 7077896 | tf_op jit(solution)/shard_map/ppermute | solution.py:411
  157.5 38.4 %all-to-all-start.1 = ((bf16[64,16,1152]{2,1,0:T(8,128)(2,1)}), bf16[64,16,1152]{2,1,0:T(8,128)(2,1)}, u32[]{:S(2)}, u32[]{:S(2)}) async-start(bf16[64,16,1152]{2,1,0:T(8,128)(2,1)} %add.52), calls=%async_computation.1 | async-start | bytes 4718592 | tf_op jit(solution)/shard_map/all_to_all | solution.py:448
  173.3 2.7 %collective-permute-start.20 = (bf16[512,1024]{1,0:T(8,128)(2,1)S(1)}, bf16[512,1024]{1,0:T(8,128)(2,1)S(1)}, u32[]{:S(2)}, u32[]{:S(2)}) collective-permute-start(bf16[512,1024]{1,0:T(8,128)(2,1)S(1)} %get-tuple-element.75), channel_id=1, source_target_pairs={{0,1},{1,0},{2,3},{3,2},{4,5},{5,4},{6,7},{7,6},{8,9},{9,8},{10,11... | collective-permute-start | bytes 3145736 | tf_op jit(solution)/shard_map/ppermute | solution.py:411
  176.5 25.6 %collective-permute-start.21 = (bf16[128,1024]{1,0:T(8,128)(2,1)S(1)}, bf16[128,1024]{1,0:T(8,128)(2,1)S(1)}, u32[]{:S(2)}, u32[]{:S(2)}) collective-permute-start(bf16[128,1024]{1,0:T(8,128)(2,1)S(1)} %get-tuple-element.78), channel_id=1, source_target_pairs={{0,2},{1,3},{2,4},{3,5},{4,6},{5,7},{6,0},{7,1},{8,10},{9,11},{10,... | collective-permute-start | bytes 786440 | tf_op jit(solution)/shard_map/ppermute | solution.py:415
  177.1 25.0 %collective-permute-start.23 = (bf16[128,1024]{1,0:T(8,128)(2,1)S(1)}, bf16[128,1024]{1,0:T(8,128)(2,1)S(1)}, u32[]{:S(2)}, u32[]{:S(2)}) collective-permute-start(bf16[128,1024]{1,0:T(8,128)(2,1)S(1)} %get-tuple-element.79), channel_id=1, source_target_pairs={{0,6},{1,7},{2,0},{3,1},{4,2},{5,3},{6,4},{7,5},{8,14},{9,15},{10,... | collective-permute-start | bytes 786440 | tf_op jit(solution)/shard_map/ppermute | solution.py:415
  179.8 22.3 %collective-permute-start.22 = (bf16[128,1024]{1,0:T(8,128)(2,1)S(1)}, bf16[128,1024]{1,0:T(8,128)(2,1)S(1)}, u32[]{:S(2)}, u32[]{:S(2)}) collective-permute-start(bf16[128,1024]{1,0:T(8,128)(2,1)S(1)} %get-tuple-element.80), channel_id=1, source_target_pairs={{0,4},{1,5},{2,6},{3,7},{4,0},{5,1},{6,2},{7,3},{8,12},{9,13},{10,... | collective-permute-start | bytes 786440 | tf_op jit(solution)/shard_map/ppermute | solution.py:415
  198.6 9.5 %all-to-all-start.2 = ((bf16[4,16,1152]{2,1,0:T(8,128)(2,1)}), bf16[4,16,1152]{2,1,0:T(8,128)(2,1)S(1)}, u32[]{:S(2)}, u32[]{:S(2)}) async-start(bf16[4,16,1152]{2,1,0:T(8,128)(2,1)} %reduce_sum.31), calls=%async_computation.2 | async-start | bytes 294912 | tf_op jit(solution)/shard_map/all_to_all | solution.py:457
  (14 other events, 84.9 us)
